TPU v7x, 32 devices: a whole 2x2x4 slice. The times are simulated.
32 devices in a mesh: lag: 16 (over z, y, x), col: 2 (over core).
Axes of the slice: x: 2, y: 2, z: 4, core: 2. Of those that a mesh axis runs over, the one named last changes fastest.
Arguments:
- tap_matrices: bfloat16 [16, 1024, 2048], P('lag', None, 'col'), may hold values from -0.125 to 0.125
- density_history: bfloat16 [64, 2048, 128], P('lag', 'col'), may hold values from -6 to 6
- offsets: int32 [16], P('lag'), may hold values from 0 to 3
- column_slots: int32 [2, 128], P('col'), may hold values from 0 to 127, each once within a row
Outputs:
- history_sum: float32 [16, 1024, 3, 128], P('lag', 'col')
Inputs may be any that keep to these rules, and one draw needn't show every extreme that they name: Section s reads history slots s * 4 + offsets[s] to s * 4 + offsets[s] + 2. `column_slots`: each row is a permutation of the 128 stored columns.
All inputs are finite; a program needn't handle non-finite values.
Results may differ from a plain program's by a relative error of at most 0.0003.
Values may be sent and summed in bfloat16 or wider, within the bound.
No kernel may reach another device: no remote copies, remote signals or barrier semaphores. Data moves between devices by JAX's collectives and lax.ppermute only.
A program may use at most 128 MiB of HBM per device.

v0:
```python
import jax
import jax.numpy as jnp
from jax import lax
from jax.sharding import PartitionSpec as P

TICKS = 3


def shifted(value, axis, steps):
    count = lax.axis_size(axis)
    initial, last = (max(0, -steps), min(count, count - steps))
    return lax.ppermute(value, axis, [(source, source + steps) for source in range(initial, last)])


def carried_in(part, axis, combine, identity):
    place = lax.axis_index(axis)
    gathered = lax.all_gather(part, axis)
    state = jnp.zeros_like(part) + jnp.asarray(identity, part.dtype)

    def one(step, state):
        return combine(state, lax.dynamic_index_in_dim(gathered, step, 0, False))

    return lax.fori_loop(0, place, one, state)


def combine_sum(earlier, current):
    return earlier + current


def local(tap_matrices, density_history, offsets, column_slots):
    tap_matrix = tap_matrices[0]
    ordered = jnp.take(density_history, column_slots[0], axis=2)
    newer_block = shifted(ordered[: TICKS - 1], "lag", -1)
    window = jnp.concatenate([ordered, newer_block], axis=0)
    densities = lax.dynamic_slice_in_dim(window, offsets[0], TICKS, 0)
    reduced = lax.psum_scatter(
        jnp.einsum("mc,tce->mte", tap_matrix, densities, preferred_element_type=jnp.float32),
        "col",
        scatter_dimension=0,
        tiled=True,
    )
    earlier = carried_in(reduced, "lag", combine_sum, jnp.zeros_like(reduced))
    history_sum = earlier + reduced
    return history_sum[None]


def solution(mesh):
    return jax.shard_map(
        local,
        mesh=mesh,
        in_specs=(P("lag", None, "col"), P("lag", "col", None), P("lag"), P("col", None)),
        out_specs=P("lag", "col", None, None),
        check_vma=False,
    )
```

profile of v0, /device:TPU:31, one launch (start us, length us, event | category | flops | bytes accessed | tf_op | source)
XLA Modules:
  0.0 254.6 jit_solution(3513210604475420867)
XLA Ops:
  6.5 0.8 fusion.8
  7.3 0.7 compare_and_fusion
  8.0 2.7 %copy.8 = bf16[4,1024,128]{1,0,2:T(4,128)(2,1)} copy(bf16[4,1024,128]{2,1,0:T(8,128)(2,1)} %param.7) | data formatting | bytes 2097152 | tf_op args[1]
  10.7 2.7 %gather_fusion = bf16[128,4,1024]{2,1,0:T(4,128)(2,1)S(1)} fusion(bf16[4,1024,128]{1,0,2:T(4,128)(2,1)} %copy.8, s32[1024]{0:T(1024)S(1)} %pad_clamp_fusion), kind=kCustom, calls=%fused_computation | custom fusion | bytes 2097664 | tf_op jit(solution)/shard_map/jit(_take)/gather | solution.py:32
  13.4 0.7 fusion.5
  14.1 1.0 copy-done.1
  15.1 2.2 collective-permute-start
  17.9 9.9 %collective-permute-done = bf16[2,1024,128]{1,2,0:T(8,128)(2,1)S(1)} collective-permute-done((bf16[2,1024,128]{1,2,0:T(8,128)(2,1)S(1)}, bf16[2,1024,128]{1,2,0:T(8,128)(2,1)S(1)}, u32[]{:S(2)}, u32[]{:S(2)}) %collective-permute-start) | collective-permute-done | bytes 524320 | tf_op jit(solution)/shard_map/ppermute | solution.py:12
  27.8 3.3 %fusion.2 = f32[1024,3,128]{0,2,1:T(8,128)} fusion(bf16[1,1024,1024]{2,1,0:T(8,128)(2,1)S(1)} %copy-done, s32[]{:T(128)S(6)} %select_n.30, bf16[4,1024,128]{1,2,0:T(8,128)(2,1)} %copy-done.1, bf16[2,1024,128]{1,2,0:T(8,128)(2,1)S(1)} %collective-permute-done), kind=kOutput, calls=%fused_computation.6 | convolution fusion | flops 805699584 | bytes 5242884 | tf_op jit(solution)/shard_map/mc,tce->mte/dot_general | solution.py:37
  31.2 14.3 %reduce-scatter.2.cloned.1.call-done = f32[512,3,128]{0,2,1:T(8,128)} async-done(((f32[1024,3,128]{0,2,1:T(8,128)}), f32[512,3,128]{0,2,1:T(8,128)}) %reduce-scatter.2.cloned.1.call-update) | async-done | bytes 786448 | tf_op jit(solution)/shard_map/reduce_scatter | solution.py:36
  45.5 156.9 %all-gather.3.cloned.1.call-done = f32[8192,3,128]{0,2,1:T(8,128)} async-done(((f32[512,3,128]{0,2,1:T(8,128)}), f32[8192,3,128]{0,2,1:T(8,128)}) %all-gather.3.cloned.1.call-update) | async-done | bytes 12582928 | tf_op jit(solution)/shard_map/all_gather | solution.py:17
  202.5 17.4 %copy.13 = f32[8192,3,128]{2,1,0:T(4,128)} copy(f32[8192,3,128]{0,2,1:T(8,128)} %all-gather.3.cloned.1.call-done) | data formatting | bytes 25165824 | tf_op jit(solution)/shard_map/while | solution.py:23
  219.9 0.1 broadcast_in_dim.16
  220.0 23.9 %while.10 = (s32[]{:T(128)}, f32[512,3,128]{2,1,0:T(4,128)S(1)}, s32[]{:T(128)}, f32[16,512,3,128]{3,2,1,0:T(4,128)}, s32[]{:T(128)}, /*index=5*/s32[]{:T(128)}, s32[]{:T(128)}) while((s32[]{:T(128)}, f32[512,3,128]{2,1,0:T(4,128)S(1)}, s32[]{:T(128)}, f32[16,512,3,128]{3,2,1,0:T(4,128)}, s32[]{:T(128)}, /*index=5*/s32[]{:T(128)}, ...), condition=%wide.region_2.3_spmd, body=%wide.region_1.2_spmd.sunk | while | flops 196613 | bytes 2359411 | solution.py:23
  220.0 1.6 bitcast_add_fusion.2
  221.6 1.6 bitcast_add_fusion.2
  223.2 1.6 bitcast_add_fusion.2
  224.8 1.6 bitcast_add_fusion.2
  226.4 1.6 bitcast_add_fusion.2
  228.0 1.6 bitcast_add_fusion.2
  229.6 1.6 bitcast_add_fusion.2
  231.2 1.6 bitcast_add_fusion.2
  232.8 1.6 bitcast_add_fusion.2
  234.4 1.6 bitcast_add_fusion.2
  236.0 1.6 bitcast_add_fusion.2
  237.6 1.6 bitcast_add_fusion.2
  239.2 1.6 bitcast_add_fusion.2
  240.7 1.6 bitcast_add_fusion.2
  242.3 1.6 bitcast_add_fusion.2
  243.9 1.2 copy.11
  245.1 1.5 add_bitcast_fusion
  246.6 1.1 copy.12
  (9 shorter events, 0.1 us)
Async XLA Ops:
  6.5 21.3 %copy-start = (bf16[1,1024,1024]{2,1,0:T(8,128)(2,1)S(1)}, bf16[1,1024,1024]{2,1,0:T(8,128)(2,1)}, u32[]{:S(2)}) copy-start(bf16[1,1024,1024]{2,1,0:T(8,128)(2,1)} %param.6) | copy-start | bytes 6291460
  6.5 39.0 %reduce-scatter.2.cloned.1.call-start = ((), (), s32[]{:S(2)}) async-start(), calls=%async_computation.1 | async-start | bytes 2359296 | tf_op jit(solution)/shard_map/reduce_scatter | solution.py:36
  14.1 1.0 copy-start.1
  15.1 12.7 %collective-permute-start = (bf16[2,1024,128]{1,2,0:T(8,128)(2,1)S(1)}, bf16[2,1024,128]{1,2,0:T(8,128)(2,1)S(1)}, u32[]{:S(2)}, u32[]{:S(2)}) collective-permute-start(bf16[2,1024,128]{1,2,0:T(8,128)(2,1)S(1)} %slice.6), channel_id=1, source_target_pairs={{2,0},{4,2},{6,4},{8,6},{10,8},{12,10},{14,12},{16,14},{18,16},{20... | collective-permute-start | bytes 1572872 | tf_op jit(solution)/shard_map/ppermute | solution.py:12
  31.1 171.3 %all-gather.3.cloned.1.call-start = ((), (), s32[]{:S(2)}) async-start(), calls=%async_computation.2 | async-start | bytes 13369344 | tf_op jit(solution)/shard_map/all_gather | solution.py:17
Sparse Core Ops, SparseCore 0:
  31.2 14.2 reduce-scatter.1
  48.6 153.7 all-gather.2
where the time goes:
time: 256 us; the launch traced here: 255 us
  waiting for transfers between devices  181 us (71%)
  other arithmetic  27.2 us (11%)
  local copies, waits for them, and re-layouts  26.2 us (10%)
  between operations  14.1 us (6%)
  matrix products  3.3 us (1%)
    all_gather x1, waiting for transfers between devices, carried_in(): gathered = lax.all_gather(part, axis)  157 us
    add x15, other arithmetic, combine_sum(): return earlier + current  23.5 us
    while x2, local copies, waits for them, and re-layouts, carried_in(): return lax.fori_loop(0, place, one, state)  18.6 us
    reduce_scatter x1, waiting for transfers between devices, local(): lax.psum_scatter(jnp.einsum('mc,tce->mte', tap_matrix, densities, preferr...  14.3 us
    ppermute x1, waiting for transfers between devices, shifted(): lax.ppermute(value, axis, [(source, source + steps) for source in range(i...  9.88 us
  transfers between devices with their start and end apart: 3, of which 3 were waited for; matrix products, arithmetic and copies ran while one was open for 0% of the time, Pallas kernels for 0%

commit v1 on v0

v1 whole, which is shorter than its diff:
```python
import functools

import jax
import jax.numpy as jnp
from jax import lax
from jax.experimental import pallas as pl
from jax.experimental.pallas import tpu as pltpu
from jax.sharding import PartitionSpec as P

TICKS = 3
INNER = 4
VMEM = pl.BlockSpec(memory_space=pltpu.VMEM)
SMEM = pl.BlockSpec(memory_space=pltpu.SMEM)
LIMIT = pltpu.CompilerParams(vmem_limit_bytes=40 * 2**20)


def call(kernel, out_shape, ins, scratch=()):
    return pl.pallas_call(
        kernel,
        out_shape=out_shape,
        in_specs=[SMEM if a.ndim == 1 else VMEM for a in ins],
        out_specs=jax.tree.map(lambda _: VMEM, out_shape),
        scratch_shapes=list(scratch),
        compiler_params=LIMIT,
    )(*ins)


def swapped(value, axis, mask):
    count = lax.axis_size(axis)
    return lax.ppermute(value, axis, [(i, i ^ mask) for i in range(count)])


def pack(x, ref):
    half = x.shape[1] // 2
    high = jnp.maximum(jnp.max(jnp.abs(x), axis=1, keepdims=True), 2.0**-100)
    power = jnp.floor(jnp.log2(high)) + 1.0
    q = jnp.clip(jnp.round(x * jnp.exp2(15.0 - power)), -32768.0, 32767.0).astype(jnp.int32)
    words = (q[:, :half] & 0xFFFF) | (q[:, half:] << 16)
    for t in range(TICKS):
        ref[t * half : (t + 1) * half, :] = words[t]
    scales = power.astype(jnp.int32)
    tail = jnp.concatenate([scales[t] for t in range(TICKS)] + [jnp.zeros((8 - TICKS, x.shape[2]), jnp.int32)], axis=0)
    ref[TICKS * half : TICKS * half + 8, :] = tail


def unpack(ref, half):
    tail = ref[TICKS * half : TICKS * half + 8, :].astype(jnp.float32)
    unit = jnp.exp2(tail - 15.0)
    ticks = []
    for t in range(TICKS):
        words = ref[t * half : (t + 1) * half, :]
        both = jnp.concatenate([(words << 16) >> 16, words >> 16], axis=0)
        ticks.append(both.astype(jnp.float32) * unit[t : t + 1])
    return jnp.stack(ticks)


def product_kernel(n_col, where, offset, taps, own, newer, slots, keep, *rest):
    sends, window = rest[:-1], rest[-1]
    slots_own, source, width = own.shape
    rows = keep.shape[1]
    place, last = where[0], where[1]
    chosen = lax.broadcasted_iota(jnp.int32, (width, width), 0) == slots[...]
    chosen = chosen.astype(jnp.float32).astype(jnp.bfloat16)
    for t in range(TICKS):
        slot = offset[0] + t
        lanes = slice(t * width, (t + 1) * width)

        @pl.when(slot < slots_own)
        def _():
            part = jnp.dot(own[jnp.minimum(slot, slots_own - 1)], chosen, preferred_element_type=jnp.float32)
            window[:, lanes] = part.astype(jnp.bfloat16)

        @pl.when(slot >= slots_own)
        def _():
            part = jnp.dot(newer[jnp.maximum(slot - slots_own, 0)], chosen, preferred_element_type=jnp.float32)
            window[:, lanes] = jnp.where(last == 1, 0.0, part).astype(jnp.bfloat16)

    step = min(rows, 256)
    for k, out in enumerate((keep, *sends)):
        for start in range(0, rows, step):
            first = pl.multiple_of((place ^ k) * rows + start, step)
            result = jnp.dot(taps[pl.ds(first, step), :], window[...], preferred_element_type=jnp.float32)
            for t in range(TICKS):
                out[t, start : start + step, :] = result[:, t * width : (t + 1) * width]


def split_kernel(n_col, where, *refs):
    parts, (own, mine, *sends) = refs[:n_col], refs[n_col:]
    total = parts[0][...]
    for part in parts[1:]:
        total = total + part[...]
    own[...] = total
    piece = own.shape[1] // INNER
    for k, out in enumerate((mine, *sends)):
        first = pl.multiple_of((where[2] ^ k) * piece, piece)
        value = own[:, pl.ds(first, piece), :]
        if k:
            pack(value, out)
        else:
            out[...] = value


def total_kernel(mine, *refs):
    received, out = refs[:-1], refs[-1]
    half = mine.shape[1] // 2
    total = mine[...]
    for ref in received:
        total = total + unpack(ref, half)
    pack(total, out)


def prefix_kernel(n_outer, where, mine, *refs):
    received, totals, (base, *sends) = refs[: INNER - 1], refs[INNER - 1 : INNER + n_outer - 2], refs[INNER + n_outer - 2 :]
    half = mine.shape[1] // 2
    place, group = where[2], where[3]
    earlier = jnp.zeros(mine.shape, jnp.float32)
    for k, ref in enumerate(totals, 1):
        earlier = earlier + jnp.where((group ^ k) < group, unpack(ref, half), 0.0)
    terms = [mine[...]] + [unpack(ref, half) for ref in received]
    for k, out in enumerate((base, *sends)):
        value = earlier
        for m, term in enumerate(terms):
            if m != k:
                value = value + jnp.where((place ^ m) < (place ^ k), term, 0.0)
        if k:
            pack(value, out)
        else:
            out[...] = value


def finish_kernel(where, own, base, *refs):
    received, out = refs[:-1], refs[-1]
    piece = base.shape[1]
    for k, ref in enumerate((base, *received)):
        first = pl.multiple_of((where[2] ^ k) * piece, piece)
        older = unpack(ref, piece // 2) if k else ref[...]
        out[:, pl.ds(first, piece), :] = own[:, pl.ds(first, piece), :] + older


def local(tap_matrices, density_history, offsets, column_slots):
    n_lag, n_col = lax.axis_size("lag"), lax.axis_size("col")
    n_outer = n_lag // INNER
    lag, col = lax.axis_index("lag"), lax.axis_index("col")
    where = jnp.stack([col, (lag == n_lag - 1).astype(jnp.int32), lag % INNER, lag // INNER]).astype(jnp.int32)
    taps = tap_matrices[0]
    unknowns, source = taps.shape
    width = column_slots.shape[1]
    rows = unknowns // n_col
    piece = rows // INNER
    f32 = functools.partial(jax.ShapeDtypeStruct, dtype=jnp.float32)
    packed = jax.ShapeDtypeStruct((TICKS * piece // 2 + 8, width), jnp.int32)

    newer = lax.ppermute(density_history[: TICKS - 1], "lag", [(i, (i - 1) % n_lag) for i in range(n_lag)])
    products = call(
        functools.partial(product_kernel, n_col),
        [f32((TICKS, rows, width))] * n_col,
        [where, offsets, taps, density_history, newer, column_slots],
        [pltpu.VMEM((source, TICKS * width), jnp.bfloat16)],
    )
    others = [swapped(value, "col", k) for k, value in enumerate(products[1:], 1)]
    own, mine, *sends = call(
        functools.partial(split_kernel, n_col),
        [f32((TICKS, rows, width)), f32((TICKS, piece, width))] + [packed] * (INNER - 1),
        [where, products[0], *others],
    )
    received = [swapped(value, "lag", k) for k, value in enumerate(sends, 1)]
    [total] = call(total_kernel, [packed], [mine, *received])
    totals = [swapped(total, "lag", k * INNER) for k in range(1, n_outer)]
    base, *sends = call(
        functools.partial(prefix_kernel, n_outer),
        [f32((TICKS, piece, width))] + [packed] * (INNER - 1),
        [where, mine, *received, *totals],
    )
    received = [swapped(value, "lag", k) for k, value in enumerate(sends, 1)]
    [history_sum] = call(finish_kernel, [f32((TICKS, rows, width))], [where, own, base, *received])
    return jnp.transpose(history_sum, (1, 0, 2))[None]


def solution(mesh):
    return jax.shard_map(
        local,
        mesh=mesh,
        in_specs=(P("lag", None, "col"), P("lag", "col", None), P("lag"), P("col", None)),
        out_specs=P("lag", "col", None, None),
        check_vma=False,
    )
```

time: 256 us -> 59.1 us (0.23)
  the two profiles are of different devices: /device:TPU:31 before, /device:TPU:0 now
where the time goes in v1:
time: 59.1 us; the launch traced here: 58.8 us
  waiting for transfers between devices  27.3 us (46%)
  starting transfers between devices  20.3 us (34%)
  Pallas kernels  5.94 us (10%)
  local copies, waits for them, and re-layouts  4.55 us (8%)
  between operations  0.71 us (1%)
    ppermute x10, waiting for transfers between devices, swapped(): return lax.ppermute(value, axis, [(i, i ^ mask) for i in range(count)])  16.8 us
    ppermute x10, starting transfers between devices, swapped(): return lax.ppermute(value, axis, [(i, i ^ mask) for i in range(count)])  13.3 us
    ppermute x1, waiting for transfers between devices, local(): lax.ppermute(density_history[:TICKS - 1], 'lag', [(i, (i - 1) % n_lag) fo...  10.4 us
    ppermute x1, starting transfers between devices, local(): lax.ppermute(density_history[:TICKS - 1], 'lag', [(i, (i - 1) % n_lag) fo...  6.98 us
    pallas_call x5, Pallas kernels, call(): pl.pallas_call(kernel, out_shape=out_shape, in_specs=[SMEM if a.ndim == 1...  5.94 us
    unnamed x6, local copies, waits for them, and re-layouts  3.47 us
  transfers between devices with their start and end apart: 11, of which 9 were waited for; matrix products, arithmetic and copies ran while one was open for 0% of the time, Pallas kernels for 0%

profile of v1, /device:TPU:0, one launch (start us, length us, event | category | flops | bytes accessed | tf_op | source)
XLA Modules:
  0.0 58.8 jit_solution(12650075144401400805)
XLA Ops:
  0.0 1.1 %slice.3 = bf16[2,1024,128]{2,1,0:T(8,128)(2,1)S(1)} slice(bf16[4,1024,128]{2,1,0:T(8,128)(2,1)} %own.1), slice={[0:2], [0:1024], [0:128]} | slice | bytes 1048576 | tf_op jit(solution)/shard_map/slice | solution.py:153
  1.1 7.0 %collective-permute-start = (bf16[2,1024,128]{2,1,0:T(8,128)(2,1)S(1)}, bf16[2,1024,128]{2,1,0:T(8,128)(2,1)S(1)}, u32[]{:S(2)}, u32[]{:S(2)}) collective-permute-start(bf16[2,1024,128]{2,1,0:T(8,128)(2,1)S(1)} %slice.3), channel_id=1, source_target_pairs={{0,30},{2,0},{4,2},{6,4},{8,6},{10,8},{12,10},{14,12},{16,14},{18,... | collective-permute-start | bytes 1572872 | tf_op jit(solution)/shard_map/ppermute | solution.py:153
  8.7 0.1 pad_add_fusion.where
  8.8 10.4 %collective-permute-done.newer = bf16[2,1024,128]{2,1,0:T(8,128)(2,1)S(1)} collective-permute-done((bf16[2,1024,128]{2,1,0:T(8,128)(2,1)S(1)}, bf16[2,1024,128]{2,1,0:T(8,128)(2,1)S(1)}, u32[]{:S(2)}, u32[]{:S(2)}) %collective-permute-start) | collective-permute-done | bytes 524320 | tf_op jit(solution)/shard_map/ppermute | solution.py:153
  19.2 1.2 %copy-done = bf16[4,1024,128]{2,1,0:T(8,128)(2,1)S(1)} copy-done((bf16[4,1024,128]{2,1,0:T(8,128)(2,1)S(1)}, bf16[4,1024,128]{2,1,0:T(8,128)(2,1)}, u32[]{:S(2)}) %copy-start) | copy-done | bytes 1048600
  20.5 1.6 %copy-done.1 = bf16[1,1024,1024]{2,1,0:T(8,128)(2,1)S(1)} copy-done((bf16[1,1024,1024]{2,1,0:T(8,128)(2,1)S(1)}, bf16[1,1024,1024]{2,1,0:T(8,128)(2,1)}, u32[]{:S(2)}) %copy-start.1) | copy-done | bytes 2097176
  22.1 0.7 %copy-done.2 = s32[1,128]{1,0:T(1,128)S(1)} copy-done((s32[1,128]{1,0:T(1,128)S(1)}, s32[1,128]{1,0:T(1,128)}, u32[]{:S(2)}) %copy-start.2) | copy-done | bytes 536
  22.7 2.4 %shard_map.46 = (f32[3,512,128]{2,1,0:T(8,128)S(1)}, f32[3,512,128]{2,1,0:T(8,128)S(1)}) custom-call(s32[4]{0:T(128)S(1)} %pad_add_fusion.where, s32[1]{0:T(128)S(6)} %copy.5.offset, bf16[1024,1024]{1,0:T(8,128)(2,1)S(1)} %bitcast.8, bf16[4,1024,128]{2,1,0:T(8,128)(2,1)S(1)} %copy-done, bf16[2,1024,128]{2,1,0:T(8,128)(2,1)S(1)} %collective-permute-done.newer, ...), custom_call_target="tpu_custom_call" | custom-call | tf_op jit(solution)/shard_map/pallas_call | solution.py:18
  25.2 0.1 collective-permute-start.1
  25.2 2.3 %collective-permute-done.1.refs_1_ = f32[3,512,128]{2,1,0:T(8,128)S(1)} collective-permute-done((f32[3,512,128]{2,1,0:T(8,128)S(1)}, f32[3,512,128]{2,1,0:T(8,128)S(1)}, u32[]{:S(2)}, u32[]{:S(2)}) %collective-permute-start.1) | collective-permute-done | bytes 786464 | tf_op jit(solution)/shard_map/ppermute | solution.py:30
  27.5 0.8 %shard_map.47 = (f32[3,512,128]{2,1,0:T(8,128)S(1)}, f32[3,128,128]{2,1,0:T(8,128)S(1)}, s32[200,128]{1,0:T(8,128)S(1)}, s32[200,128]{1,0:T(8,128)S(1)}, s32[200,128]{1,0:T(8,128)S(1)}) custom-call(s32[4]{0:T(128)S(1)} %pad_add_fusion.where, f32[3,512,128]{2,1,0:T(8,128)S(1)} %get-tuple-element.16.refs_0_, f32[3,512,128]{2,1,0:T(8,128)S(1)} %collective-permute-done.1.refs_1_), custom_call_target="tpu_custom_call" | custom-call | tf_op jit(solution)/shard_map/pallas_call | solution.py:18
  28.3 0.1 collective-permute-start.2
  28.4 1.8 %collective-permute-start.3 = (s32[200,128]{1,0:T(8,128)S(1)}, s32[200,128]{1,0:T(8,128)S(1)}, u32[]{:S(2)}, u32[]{:S(2)}) collective-permute-start(s32[200,128]{1,0:T(8,128)S(1)} %get-tuple-element.21), channel_id=1, source_target_pairs={{0,4},{2,6},{4,0},{6,2},{8,12},{10,14},{12,8},{14,10},{16,20},{18,... | collective-permute-start | bytes 307208 | tf_op jit(solution)/shard_map/ppermute | solution.py:30
  30.2 1.7 %collective-permute-start.4 = (s32[200,128]{1,0:T(8,128)S(1)}, s32[200,128]{1,0:T(8,128)S(1)}, u32[]{:S(2)}, u32[]{:S(2)}) collective-permute-start(s32[200,128]{1,0:T(8,128)S(1)} %get-tuple-element.22), channel_id=1, source_target_pairs={{0,6},{2,4},{4,2},{6,0},{8,14},{10,12},{12,10},{14,8},{16,22},{18,... | collective-permute-start | bytes 307208 | tf_op jit(solution)/shard_map/ppermute | solution.py:30
  31.9 2.2 %collective-permute-done.2.refs_0_ = s32[200,128]{1,0:T(8,128)S(1)} collective-permute-done((s32[200,128]{1,0:T(8,128)S(1)}, s32[200,128]{1,0:T(8,128)S(1)}, u32[]{:S(2)}, u32[]{:S(2)}) %collective-permute-start.2) | collective-permute-done | bytes 102432 | tf_op jit(solution)/shard_map/ppermute | solution.py:30
  34.1 0.4 collective-permute-done.3.refs_1_
  34.5 1.3 %collective-permute-done.4.refs_2_ = s32[200,128]{1,0:T(8,128)S(1)} collective-permute-done((s32[200,128]{1,0:T(8,128)S(1)}, s32[200,128]{1,0:T(8,128)S(1)}, u32[]{:S(2)}, u32[]{:S(2)}) %collective-permute-start.4) | collective-permute-done | bytes 102432 | tf_op jit(solution)/shard_map/ppermute | solution.py:30
  35.8 0.2 shard_map.48
  35.9 5.5 %collective-permute-start.7 = (s32[200,128]{1,0:T(8,128)S(1)}, s32[200,128]{1,0:T(8,128)S(1)}, u32[]{:S(2)}, u32[]{:S(2)}) collective-permute-start(s32[200,128]{1,0:T(8,128)S(1)} %shard_map.48), channel_id=1, source_target_pairs={{0,24},{2,26},{4,28},{6,30},{8,16},{10,18},{12,20},{14,22},{16,8},... | collective-permute-start | bytes 307208 | tf_op jit(solution)/shard_map/ppermute | solution.py:30
  41.4 0.0 collective-permute-start.6
  41.4 0.6 %collective-permute-start.5 = (s32[200,128]{1,0:T(8,128)S(1)}, s32[200,128]{1,0:T(8,128)S(1)}, u32[]{:S(2)}, u32[]{:S(2)}) collective-permute-start(s32[200,128]{1,0:T(8,128)S(1)} %shard_map.48), channel_id=1, source_target_pairs={{0,8},{2,10},{4,12},{6,14},{8,0},{10,2},{12,4},{14,6},{16,24},{18,... | collective-permute-start | bytes 307208 | tf_op jit(solution)/shard_map/ppermute | solution.py:30
  42.0 2.3 %collective-permute-done.7.refs_5_ = s32[200,128]{1,0:T(8,128)S(1)} collective-permute-done((s32[200,128]{1,0:T(8,128)S(1)}, s32[200,128]{1,0:T(8,128)S(1)}, u32[]{:S(2)}, u32[]{:S(2)}) %collective-permute-start.7) | collective-permute-done | bytes 102432 | tf_op jit(solution)/shard_map/ppermute | solution.py:30
  44.4 3.9 %collective-permute-done.6.refs_4_ = s32[200,128]{1,0:T(8,128)S(1)} collective-permute-done((s32[200,128]{1,0:T(8,128)S(1)}, s32[200,128]{1,0:T(8,128)S(1)}, u32[]{:S(2)}, u32[]{:S(2)}) %collective-permute-start.6) | collective-permute-done | bytes 102432 | tf_op jit(solution)/shard_map/ppermute | solution.py:30
  48.3 0.0 collective-permute-done.5.refs_3_
  48.3 1.0 %shard_map.49 = (f32[3,128,128]{2,1,0:T(8,128)S(1)}, s32[200,128]{1,0:T(8,128)S(1)}, s32[200,128]{1,0:T(8,128)S(1)}, s32[200,128]{1,0:T(8,128)S(1)}) custom-call(s32[4]{0:T(128)S(1)} %pad_add_fusion.where, f32[3,128,128]{2,1,0:T(8,128)S(1)} %get-tuple-element.19.mine, s32[200,128]{1,0:T(8,128)S(1)} %collective-permute-done.2.refs_0_, ...), custom_call_target="tpu_custom_call" | custom-call | tf_op jit(solution)/shard_map/pallas_call | solution.py:18
  49.3 1.3 %collective-permute-start.8 = (s32[200,128]{1,0:T(8,128)S(1)}, s32[200,128]{1,0:T(8,128)S(1)}, u32[]{:S(2)}, u32[]{:S(2)}) collective-permute-start(s32[200,128]{1,0:T(8,128)S(1)} %get-tuple-element.24), channel_id=1, source_target_pairs={{0,2},{2,0},{4,6},{6,4},{8,10},{10,8},{12,14},{14,12},{16,18},{18,... | collective-permute-start | bytes 307208 | tf_op jit(solution)/shard_map/ppermute | solution.py:30
  50.6 0.6 %collective-permute-start.9 = (s32[200,128]{1,0:T(8,128)S(1)}, s32[200,128]{1,0:T(8,128)S(1)}, u32[]{:S(2)}, u32[]{:S(2)}) collective-permute-start(s32[200,128]{1,0:T(8,128)S(1)} %get-tuple-element.25), channel_id=1, source_target_pairs={{0,4},{2,6},{4,0},{6,2},{8,12},{10,14},{12,8},{14,10},{16,20},{18,... | collective-permute-start | bytes 307208 | tf_op jit(solution)/shard_map/ppermute | solution.py:30
  51.2 1.6 %collective-permute-start.10 = (s32[200,128]{1,0:T(8,128)S(1)}, s32[200,128]{1,0:T(8,128)S(1)}, u32[]{:S(2)}, u32[]{:S(2)}) collective-permute-start(s32[200,128]{1,0:T(8,128)S(1)} %get-tuple-element.26), channel_id=1, source_target_pairs={{0,6},{2,4},{4,2},{6,0},{8,14},{10,12},{12,10},{14,8},{16,22},{18,... | collective-permute-start | bytes 307208 | tf_op jit(solution)/shard_map/ppermute | solution.py:30
  52.9 1.6 %collective-permute-done.8.refs_0_ = s32[200,128]{1,0:T(8,128)S(1)} collective-permute-done((s32[200,128]{1,0:T(8,128)S(1)}, s32[200,128]{1,0:T(8,128)S(1)}, u32[]{:S(2)}, u32[]{:S(2)}) %collective-permute-start.8) | collective-permute-done | bytes 102432 | tf_op jit(solution)/shard_map/ppermute | solution.py:30
  54.5 2.8 %collective-permute-done.9.refs_1_ = s32[200,128]{1,0:T(8,128)S(1)} collective-permute-done((s32[200,128]{1,0:T(8,128)S(1)}, s32[200,128]{1,0:T(8,128)S(1)}, u32[]{:S(2)}, u32[]{:S(2)}) %collective-permute-start.9) | collective-permute-done | bytes 102432 | tf_op jit(solution)/shard_map/ppermute | solution.py:30
  57.3 0.0 collective-permute-done.10.refs_2_
  57.3 1.5 %shard_map.50 = f32[3,512,128]{2,1,0:T(8,128)} custom-call(s32[4]{0:T(128)S(1)} %pad_add_fusion.where, f32[3,512,128]{2,1,0:T(8,128)S(1)} %get-tuple-element.18.own, f32[3,128,128]{2,1,0:T(8,128)S(1)} %get-tuple-element.23.base, s32[200,128]{1,0:T(8,128)S(1)} %collective-permute-done.8.refs_0_, s32[200,128]{1,0:T(8,128)S(1)} %collective-permute-done.9.refs_1_, ...), custom_call_target="tpu_custom_call" | custom-call | tf_op jit(solution)/shard_map/pallas_call | solution.py:18
  (3 shorter events, 0.0 us)
Async XLA Ops:
  1.1 18.2 %collective-permute-start = (bf16[2,1024,128]{2,1,0:T(8,128)(2,1)S(1)}, bf16[2,1024,128]{2,1,0:T(8,128)(2,1)S(1)}, u32[]{:S(2)}, u32[]{:S(2)}) collective-permute-start(bf16[2,1024,128]{2,1,0:T(8,128)(2,1)S(1)} %slice.3), channel_id=1, source_target_pairs={{0,30},{2,0},{4,2},{6,4},{8,6},{10,8},{12,10},{14,12},{16,14},{18,... | collective-permute-start | bytes 1572872 | tf_op jit(solution)/shard_map/ppermute | solution.py:153
  19.2 1.2 %copy-start = (bf16[4,1024,128]{2,1,0:T(8,128)(2,1)S(1)}, bf16[4,1024,128]{2,1,0:T(8,128)(2,1)}, u32[]{:S(2)}) copy-start(bf16[4,1024,128]{2,1,0:T(8,128)(2,1)} %own.1) | copy-start | bytes 3145732
  20.5 1.6 %copy-start.1 = (bf16[1,1024,1024]{2,1,0:T(8,128)(2,1)S(1)}, bf16[1,1024,1024]{2,1,0:T(8,128)(2,1)}, u32[]{:S(2)}) copy-start(bf16[1,1024,1024]{2,1,0:T(8,128)(2,1)} %param.4) | copy-start | bytes 6291460
  22.1 0.7 %copy-start.2 = (s32[1,128]{1,0:T(1,128)S(1)}, s32[1,128]{1,0:T(1,128)}, u32[]{:S(2)}) copy-start(s32[1,128]{1,0:T(1,128)} %slots.1) | copy-start | bytes 1540
  25.2 2.4 %collective-permute-start.1 = (f32[3,512,128]{2,1,0:T(8,128)S(1)}, f32[3,512,128]{2,1,0:T(8,128)S(1)}, u32[]{:S(2)}, u32[]{:S(2)}) collective-permute-start(f32[3,512,128]{2,1,0:T(8,128)S(1)} %get-tuple-element.17), channel_id=1, source_target_pairs={{0,1},{1,0},{2,3},{3,2},{4,5},{5,4},{6,7},{7,6},{8,9},{9,8},{10,11... | collective-permute-start | bytes 2359304 | tf_op jit(solution)/shard_map/ppermute | solution.py:30
  28.3 5.8 %collective-permute-start.2 = (s32[200,128]{1,0:T(8,128)S(1)}, s32[200,128]{1,0:T(8,128)S(1)}, u32[]{:S(2)}, u32[]{:S(2)}) collective-permute-start(s32[200,128]{1,0:T(8,128)S(1)} %get-tuple-element.20), channel_id=1, source_target_pairs={{0,2},{2,0},{4,6},{6,4},{8,10},{10,8},{12,14},{14,12},{16,18},{18,... | collective-permute-start | bytes 307208 | tf_op jit(solution)/shard_map/ppermute | solution.py:30
  28.4 6.1 %collective-permute-start.3 = (s32[200,128]{1,0:T(8,128)S(1)}, s32[200,128]{1,0:T(8,128)S(1)}, u32[]{:S(2)}, u32[]{:S(2)}) collective-permute-start(s32[200,128]{1,0:T(8,128)S(1)} %get-tuple-element.21), channel_id=1, source_target_pairs={{0,4},{2,6},{4,0},{6,2},{8,12},{10,14},{12,8},{14,10},{16,20},{18,... | collective-permute-start | bytes 307208 | tf_op jit(solution)/shard_map/ppermute | solution.py:30
  30.2 5.6 %collective-permute-start.4 = (s32[200,128]{1,0:T(8,128)S(1)}, s32[200,128]{1,0:T(8,128)S(1)}, u32[]{:S(2)}, u32[]{:S(2)}) collective-permute-start(s32[200,128]{1,0:T(8,128)S(1)} %get-tuple-element.22), channel_id=1, source_target_pairs={{0,6},{2,4},{4,2},{6,0},{8,14},{10,12},{12,10},{14,8},{16,22},{18,... | collective-permute-start | bytes 307208 | tf_op jit(solution)/shard_map/ppermute | solution.py:30
  35.9 8.4 %collective-permute-start.7 = (s32[200,128]{1,0:T(8,128)S(1)}, s32[200,128]{1,0:T(8,128)S(1)}, u32[]{:S(2)}, u32[]{:S(2)}) collective-permute-start(s32[200,128]{1,0:T(8,128)S(1)} %shard_map.48), channel_id=1, source_target_pairs={{0,24},{2,26},{4,28},{6,30},{8,16},{10,18},{12,20},{14,22},{16,8},... | collective-permute-start | bytes 307208 | tf_op jit(solution)/shard_map/ppermute | solution.py:30
  41.4 6.9 %collective-permute-start.6 = (s32[200,128]{1,0:T(8,128)S(1)}, s32[200,128]{1,0:T(8,128)S(1)}, u32[]{:S(2)}, u32[]{:S(2)}) collective-permute-start(s32[200,128]{1,0:T(8,128)S(1)} %shard_map.48), channel_id=1, source_target_pairs={{0,16},{2,18},{4,20},{6,22},{8,24},{10,26},{12,28},{14,30},{16,0},... | collective-permute-start | bytes 307208 | tf_op jit(solution)/shard_map/ppermute | solution.py:30
  41.4 6.9 %collective-permute-start.5 = (s32[200,128]{1,0:T(8,128)S(1)}, s32[200,128]{1,0:T(8,128)S(1)}, u32[]{:S(2)}, u32[]{:S(2)}) collective-permute-start(s32[200,128]{1,0:T(8,128)S(1)} %shard_map.48), channel_id=1, source_target_pairs={{0,8},{2,10},{4,12},{6,14},{8,0},{10,2},{12,4},{14,6},{16,24},{18,... | collective-permute-start | bytes 307208 | tf_op jit(solution)/shard_map/ppermute | solution.py:30
  49.3 5.2 %collective-permute-start.8 = (s32[200,128]{1,0:T(8,128)S(1)}, s32[200,128]{1,0:T(8,128)S(1)}, u32[]{:S(2)}, u32[]{:S(2)}) collective-permute-start(s32[200,128]{1,0:T(8,128)S(1)} %get-tuple-element.24), channel_id=1, source_target_pairs={{0,2},{2,0},{4,6},{6,4},{8,10},{10,8},{12,14},{14,12},{16,18},{18,... | collective-permute-start | bytes 307208 | tf_op jit(solution)/shard_map/ppermute | solution.py:30
  50.6 6.7 %collective-permute-start.9 = (s32[200,128]{1,0:T(8,128)S(1)}, s32[200,128]{1,0:T(8,128)S(1)}, u32[]{:S(2)}, u32[]{:S(2)}) collective-permute-start(s32[200,128]{1,0:T(8,128)S(1)} %get-tuple-element.25), channel_id=1, source_target_pairs={{0,4},{2,6},{4,0},{6,2},{8,12},{10,14},{12,8},{14,10},{16,20},{18,... | collective-permute-start | bytes 307208 | tf_op jit(solution)/shard_map/ppermute | solution.py:30
  51.2 6.1 %collective-permute-start.10 = (s32[200,128]{1,0:T(8,128)S(1)}, s32[200,128]{1,0:T(8,128)S(1)}, u32[]{:S(2)}, u32[]{:S(2)}) collective-permute-start(s32[200,128]{1,0:T(8,128)S(1)} %get-tuple-element.26), channel_id=1, source_target_pairs={{0,6},{2,4},{4,2},{6,0},{8,14},{10,12},{12,10},{14,8},{16,22},{18,... | collective-permute-start | bytes 307208 | tf_op jit(solution)/shard_map/ppermute | solution.py:30

commit v2 on v1

v2 whole, which is shorter than its diff:
```python
import functools

import jax
import jax.numpy as jnp
from jax import lax
from jax.experimental import pallas as pl
from jax.experimental.pallas import tpu as pltpu
from jax.sharding import PartitionSpec as P

TICKS = 3
PARTS = 2
INNER = 4
VMEM = pl.BlockSpec(memory_space=pltpu.VMEM)
SMEM = pl.BlockSpec(memory_space=pltpu.SMEM)
HBM = pl.BlockSpec(memory_space=pl.ANY)
LIMIT = pltpu.CompilerParams(vmem_limit_bytes=40 * 2**20)
FULL = pltpu.CompilerParams(vmem_limit_bytes=60 * 2**20)


def call(kernel, out_shape, ins, scratch=(), outs=VMEM, params=LIMIT):
    return pl.pallas_call(
        kernel,
        out_shape=out_shape,
        in_specs=[SMEM if a.ndim == 1 else VMEM for a in ins],
        out_specs=jax.tree.map(lambda _: outs, out_shape),
        scratch_shapes=list(scratch),
        compiler_params=params,
    )(*ins)


def swapped(value, axis, mask):
    count = lax.axis_size(axis)
    return lax.ppermute(value, axis, [(i, i ^ mask) for i in range(count)])


def pack(x, ref):
    ticks, half = x.shape[0], x.shape[1] // 2
    high = jnp.maximum(jnp.max(jnp.abs(x), axis=1, keepdims=True), 2.0**-100)
    power = jnp.floor(jnp.log2(high)) + 1.0
    q = jnp.clip(jnp.round(x * jnp.exp2(15.0 - power)), -32768.0, 32767.0).astype(jnp.int32)
    words = (q[:, :half] & 0xFFFF) | (q[:, half:] << 16)
    for t in range(ticks):
        ref[t * half : (t + 1) * half, :] = words[t]
    scales = power.astype(jnp.int32)
    tail = jnp.concatenate([scales[t] for t in range(ticks)] + [jnp.zeros((8 - ticks, x.shape[2]), jnp.int32)], axis=0)
    ref[ticks * half : ticks * half + 8, :] = tail


def unpack(ref, half):
    ticks = (ref.shape[0] - 8) // half
    unit = jnp.exp2(ref[ticks * half : ticks * half + 8, :].astype(jnp.float32) - 15.0)
    values = []
    for t in range(ticks):
        words = ref[t * half : (t + 1) * half, :]
        both = jnp.concatenate([(words << 16) >> 16, words >> 16], axis=0)
        values.append(both.astype(jnp.float32) * unit[t : t + 1])
    return jnp.stack(values)


def chooser(slots):
    width = slots.shape[1]
    hit = lax.broadcasted_iota(jnp.int32, (width, width), 0) == slots[...]
    return hit.astype(jnp.float32).astype(jnp.bfloat16)


def prepare_kernel(where, offset, taps, own, slots, window, *sends):
    slots_own, _, width = own.shape
    chosen = chooser(slots)
    for t in range(TICKS):
        slot = offset[0] + t
        part = jnp.dot(own[jnp.minimum(slot, slots_own - 1)], chosen, preferred_element_type=jnp.float32)
        window[:, t * width : (t + 1) * width] = jnp.where(slot < slots_own, part, 0.0).astype(jnp.bfloat16)
    for k, out in enumerate(sends, 1):
        rows = out.shape[0]
        first = (where[0] ^ (1 + (k - 1) // PARTS)) * rows * PARTS + ((k - 1) % PARTS) * rows
        out[...] = taps[pl.ds(pl.multiple_of(first, rows), rows), :]


def base_kernel(n_col, where, taps, *refs):
    others, windows, out = refs[: (n_col - 1) * PARTS], refs[(n_col - 1) * PARTS : -1], refs[-1]
    rows, width = out.shape[1], out.shape[2]
    mine = taps[pl.ds(pl.multiple_of(where[0] * rows, rows), rows), :]
    total = jnp.dot(mine, windows[0][...], preferred_element_type=jnp.float32)
    for i, window in enumerate(windows[1:]):
        other = jnp.concatenate([ref[...] for ref in others[i * PARTS : (i + 1) * PARTS]], axis=0)
        total = total + jnp.dot(other, window[...], preferred_element_type=jnp.float32)
    for t in range(TICKS):
        out[t] = total[:, t * width : (t + 1) * width]


def late_kernel(n_col, where, offset, taps, base, *refs):
    cut = (n_col - 1) * PARTS
    others, newer, slots = refs[:cut], refs[cut : cut + n_col], refs[cut + n_col : cut + 2 * n_col]
    own, mine, *sends = refs[cut + 2 * n_col :]
    _, rows, width = base.shape
    local = taps[pl.ds(pl.multiple_of(where[0] * rows, rows), rows), :]
    total = 0.0
    for i in range(n_col):
        chosen = chooser(slots[i])
        parts = [jnp.dot(newer[i][j], chosen, preferred_element_type=jnp.float32) for j in range(TICKS - 1)]
        rhs = jnp.concatenate([part.astype(jnp.bfloat16) for part in parts], axis=1)
        lhs = jnp.concatenate([ref[...] for ref in others[(i - 1) * PARTS : i * PARTS]], axis=0) if i else local
        total = total + jnp.dot(lhs, rhs, preferred_element_type=jnp.float32)
    for t in range(TICKS):
        value = base[t]
        for j in range(t):
            used = (offset[0] + t == where[1] + j) & (where[2] == 0)
            value = value + jnp.where(used, total[:, j * width : (j + 1) * width], 0.0)
        own[t] = value
    piece = rows // INNER
    for k, out in enumerate((mine, *sends)):
        first = pl.multiple_of((where[3] ^ k) * piece, piece)
        value = own[:, pl.ds(first, piece), :]
        if k:
            pack(value, out)
        else:
            out[...] = value


def total_kernel(mine, *refs):
    received, out = refs[:-1], refs[-1]
    half = mine.shape[1] // 2
    total = mine[...]
    for ref in received:
        total = total + unpack(ref, half)
    pack(total, out)


def prefix_kernel(n_outer, where, mine, *refs):
    received, totals, (base, *sends) = refs[: INNER - 1], refs[INNER - 1 : INNER + n_outer - 2], refs[INNER + n_outer - 2 :]
    half = mine.shape[1] // 2
    place, group = where[3], where[4]
    earlier = jnp.zeros(mine.shape, jnp.float32)
    for k, ref in enumerate(totals, 1):
        earlier = earlier + jnp.where((group ^ k) < group, unpack(ref, half), 0.0)
    terms = [mine[...]] + [unpack(ref, half) for ref in received]
    for k, out in enumerate((base, *sends)):
        value = earlier
        for m, term in enumerate(terms):
            if m != k:
                value = value + jnp.where((place ^ m) < (place ^ k), term, 0.0)
        if k:
            pack(value, out)
        else:
            out[...] = value


def finish_kernel(where, own, base, *refs):
    received, (out, ready, sems) = refs[:-3], refs[-3:]
    piece = base.shape[1]
    copies = []
    for k, ref in enumerate((base, *received)):
        first = pl.multiple_of((where[3] ^ k) * piece, piece)
        older = unpack(ref, piece // 2) if k else ref[...]
        ready[k] = own[:, pl.ds(first, piece), :] + older
        copies.append(pltpu.make_async_copy(ready.at[k], out.at[:, pl.ds(first, piece), :], sems.at[k]))
        copies[-1].start()
    for copy in copies:
        copy.wait()


def among_members(values):
    order = range(len(values), 0, -1)
    arrived = {k: swapped(values[k - 1], "lag", k) for k in order}
    return [arrived[k] for k in range(1, len(values) + 1)]


def local(tap_matrices, density_history, offsets, column_slots):
    n_lag, n_col = lax.axis_size("lag"), lax.axis_size("col")
    n_outer = n_lag // INNER
    lag, col = lax.axis_index("lag"), lax.axis_index("col")
    slots_own, source, width = density_history.shape
    last = (lag == n_lag - 1).astype(jnp.int32)
    where = jnp.stack([col, jnp.int32(slots_own), last, lag & (INNER - 1), lag // INNER]).astype(jnp.int32)
    taps = tap_matrices[0]
    rows = taps.shape[0] // n_col
    piece = rows // INNER

    def f32(height):
        return jax.ShapeDtypeStruct((TICKS, height, width), jnp.float32)

    def bf16(*shape):
        return jax.ShapeDtypeStruct(shape, jnp.bfloat16)

    packed = jax.ShapeDtypeStruct((TICKS * piece // 2 + 8, width), jnp.int32)

    newer = lax.ppermute(density_history[: TICKS - 1], "lag", [(i, (i - 1) % n_lag) for i in range(n_lag)])
    window, *tap_sends = call(
        prepare_kernel,
        [bf16(source, TICKS * width)] + [bf16(rows // PARTS, source)] * ((n_col - 1) * PARTS),
        [where, offsets, taps, density_history, column_slots],
    )
    others = [swapped(value, "col", 1 + i // PARTS) for i, value in enumerate(tap_sends)]
    windows = [window] + [swapped(window, "col", k) for k in range(1, n_col)]
    [base] = call(functools.partial(base_kernel, n_col), [f32(rows)], [where, taps, *others, *windows])
    newer = [newer] + [swapped(newer, "col", k) for k in range(1, n_col)]
    slots = [column_slots] + [swapped(column_slots, "col", k) for k in range(1, n_col)]
    own, mine, *sends = call(
        functools.partial(late_kernel, n_col),
        [f32(rows), f32(piece)] + [packed] * (INNER - 1),
        [where, offsets, taps, base, *others, *newer, *slots],
    )
    received = among_members(sends)
    [total] = call(total_kernel, [packed], [mine, *received])
    totals = [swapped(total, "lag", k * INNER) for k in range(1, n_outer)]
    older, *sends = call(
        functools.partial(prefix_kernel, n_outer),
        [f32(piece)] + [packed] * (INNER - 1),
        [where, mine, *received, *totals],
    )
    received = among_members(sends)
    [history_sum] = call(
        finish_kernel,
        [f32(rows)],
        [where, own, older, *received],
        [pltpu.VMEM((INNER, TICKS, piece, width), jnp.float32), pltpu.SemaphoreType.DMA((INNER,))],
        HBM,
    )
    return jnp.transpose(history_sum, (1, 0, 2))[None]


def solution(mesh):
    return jax.shard_map(
        local,
        mesh=mesh,
        in_specs=(P("lag", None, "col"), P("lag", "col", None), P("lag"), P("col", None)),
        out_specs=P("lag", "col", None, None),
        check_vma=False,
    )
```

time: 59.1 us -> 52.8 us (0.89)
  waiting for transfers between devices: 27.3 us -> 18.5 us
  Pallas kernels: 5.94 us -> 7.43 us
  starting transfers between devices: 20.3 us -> 21.3 us
    ppermute x1, waiting for transfers between devices: 10.4 us -> 5.38 us  [local(): lax.ppermute(density_history[:TICKS - 1], 'lag', [(i, (i - 1) % n_lag) fo...]
    ppermute x10 -> x14, waiting for transfers between devices: 16.8 us -> 13.1 us  [swapped(): return lax.ppermute(value, axis, [(i, i ^ mask) for i in range(count)])]
    pallas_call x5 -> x6, Pallas kernels: 5.94 us -> 7.43 us  [call(): pl.pallas_call(kernel, out_shape=out_shape, in_specs=[SMEM if a.ndim == 1...]
    ppermute x10 -> x14, starting transfers between devices: 13.3 us -> 14.3 us  [swapped(): return lax.ppermute(value, axis, [(i, i ^ mask) for i in range(count)])]
  transfers between devices with their start and end apart: 11 -> 15, of which waited for: 9 -> 9; matrix products, arithmetic and copies ran while one was open for 0% -> 0% of each run, Pallas kernels for 0% -> 5%
where the time goes in v2:
time: 52.8 us; the launch traced here: 52.5 us
  starting transfers between devices  21.3 us (40%)
  waiting for transfers between devices  18.5 us (35%)
  Pallas kernels  7.43 us (14%)
  local copies, waits for them, and re-layouts  4.63 us (9%)
  between operations  0.74 us (1%)
    ppermute x14, starting transfers between devices, swapped(): return lax.ppermute(value, axis, [(i, i ^ mask) for i in range(count)])  14.3 us
    ppermute x14, waiting for transfers between devices, swapped(): return lax.ppermute(value, axis, [(i, i ^ mask) for i in range(count)])  13.1 us
    pallas_call x6, Pallas kernels, call(): pl.pallas_call(kernel, out_shape=out_shape, in_specs=[SMEM if a.ndim == 1...  7.43 us
    ppermute x1, starting transfers between devices, local(): lax.ppermute(density_history[:TICKS - 1], 'lag', [(i, (i - 1) % n_lag) fo...  6.98 us
    ppermute x1, waiting for transfers between devices, local(): lax.ppermute(density_history[:TICKS - 1], 'lag', [(i, (i - 1) % n_lag) fo...  5.38 us
    unnamed x6, local copies, waits for them, and re-layouts  3.47 us
    slice x1, local copies, waits for them, and re-layouts, local(): density_history[:TICKS - 1]  1.08 us
  transfers between devices with their start and end apart: 15, of which 9 were waited for; matrix products, arithmetic and copies ran while one was open for 0% of the time, Pallas kernels for 5%

profile of v2, /device:TPU:0, one launch (start us, length us, event | category | flops | bytes accessed | tf_op | source)
XLA Modules:
  0.0 52.5 jit_solution(3253545666917873589)
XLA Ops:
  0.0 1.1 %slice.3 = bf16[2,1024,128]{2,1,0:T(8,128)(2,1)S(1)} slice(bf16[4,1024,128]{2,1,0:T(8,128)(2,1)} %own.1), slice={[0:2], [0:1024], [0:128]} | slice | bytes 1048576 | tf_op jit(solution)/shard_map/slice | solution.py:187
  1.1 7.0 %collective-permute-start.3 = (bf16[2,1024,128]{2,1,0:T(8,128)(2,1)S(1)}, bf16[2,1024,128]{2,1,0:T(8,128)(2,1)S(1)}, u32[]{:S(2)}, u32[]{:S(2)}) collective-permute-start(bf16[2,1024,128]{2,1,0:T(8,128)(2,1)S(1)} %slice.3), channel_id=1, source_target_pairs={{0,30},{2,0},{4,2},{6,4},{8,6},{10,8},{12,10},{14,12},{16,14},{18,... | collective-permute-start | bytes 1572872 | tf_op jit(solution)/shard_map/ppermute | solution.py:187
  8.7 0.1 stack.23.where
  8.8 1.6 %copy-done = bf16[1,1024,1024]{2,1,0:T(8,128)(2,1)S(1)} copy-done((bf16[1,1024,1024]{2,1,0:T(8,128)(2,1)S(1)}, bf16[1,1024,1024]{2,1,0:T(8,128)(2,1)}, u32[]{:S(2)}) %copy-start) | copy-done | bytes 2097176
  10.4 1.2 %copy-done.1 = bf16[4,1024,128]{2,1,0:T(8,128)(2,1)S(1)} copy-done((bf16[4,1024,128]{2,1,0:T(8,128)(2,1)S(1)}, bf16[4,1024,128]{2,1,0:T(8,128)(2,1)}, u32[]{:S(2)}) %copy-start.1) | copy-done | bytes 1048600
  11.6 0.7 %copy-done.2 = s32[1,128]{1,0:T(1,128)S(1)} copy-done((s32[1,128]{1,0:T(1,128)S(1)}, s32[1,128]{1,0:T(1,128)}, u32[]{:S(2)}) %copy-start.2) | copy-done | bytes 536
  12.3 0.9 %shard_map.46 = (bf16[1024,384]{1,0:T(8,128)(2,1)S(1)}, bf16[256,1024]{1,0:T(8,128)(2,1)S(1)}, bf16[256,1024]{1,0:T(8,128)(2,1)S(1)}) custom-call(s32[5]{0:T(128)S(1)} %stack.23.where, s32[1]{0:T(128)S(6)} %copy.5.offset, bf16[1024,1024]{1,0:T(8,128)(2,1)S(1)} %bitcast.8, bf16[4,1024,128]{2,1,0:T(8,128)(2,1)S(1)} %copy-done.1, s32[1,128]{1,0:T(1,128)S(1)} %copy-done.2), custom_call_target="tpu_custom_call" | custom-call | tf_op jit(solution)/shard_map/pallas_call | solution.py:21
  13.3 0.5 collective-permute-start
  13.8 0.1 collective-permute-start.1
  13.9 5.4 %collective-permute-done.3.refs_2_ = bf16[2,1024,128]{2,1,0:T(8,128)(2,1)S(1)} collective-permute-done((bf16[2,1024,128]{2,1,0:T(8,128)(2,1)S(1)}, bf16[2,1024,128]{2,1,0:T(8,128)(2,1)S(1)}, u32[]{:S(2)}, u32[]{:S(2)}) %collective-permute-start.3) | collective-permute-done | bytes 524320 | tf_op jit(solution)/shard_map/ppermute | solution.py:187
  19.3 0.5 collective-permute-start.5
  19.8 1.8 %shard_map.47.base = f32[3,512,128]{2,1,0:T(8,128)S(1)} custom-call(s32[5]{0:T(128)S(1)} %stack.23.where, bf16[1024,1024]{1,0:T(8,128)(2,1)S(1)} %bitcast.9, bf16[256,1024]{1,0:T(8,128)(2,1)S(1)} %collective-permute-done.refs_0_, bf16[256,1024]{1,0:T(8,128)(2,1)S(1)} %collective-permute-done.1.refs_1_, bf16[1024,384]{1,0:T(8,128)(2,1)S(1)} %get-tuple-element.19.refs_2_, ...), custom_call_target="tpu_custom_call" | custom-call | tf_op jit(solution)/shard_map/pallas_call | solution.py:21
  21.6 2.1 %shard_map.48 = (f32[3,512,128]{2,1,0:T(8,128)S(1)}, f32[3,128,128]{2,1,0:T(8,128)S(1)}, s32[200,128]{1,0:T(8,128)S(1)}, s32[200,128]{1,0:T(8,128)S(1)}, s32[200,128]{1,0:T(8,128)S(1)}) custom-call(s32[5]{0:T(128)S(1)} %stack.23.where, s32[1]{0:T(128)S(6)} %copy.5.offset, bf16[1024,1024]{1,0:T(8,128)(2,1)S(1)} %bitcast.10, ...), custom_call_target="tpu_custom_call" | custom-call | tf_op jit(solution)/shard_map/pallas_call | solution.py:21
  23.8 1.8 %collective-permute-start.7 = (s32[200,128]{1,0:T(8,128)S(1)}, s32[200,128]{1,0:T(8,128)S(1)}, u32[]{:S(2)}, u32[]{:S(2)}) collective-permute-start(s32[200,128]{1,0:T(8,128)S(1)} %get-tuple-element.23), channel_id=1, source_target_pairs={{0,4},{2,6},{4,0},{6,2},{8,12},{10,14},{12,8},{14,10},{16,20},{18,... | collective-permute-start | bytes 307208 | tf_op jit(solution)/shard_map/ppermute | solution.py:33
  25.5 1.7 %collective-permute-start.8 = (s32[200,128]{1,0:T(8,128)S(1)}, s32[200,128]{1,0:T(8,128)S(1)}, u32[]{:S(2)}, u32[]{:S(2)}) collective-permute-start(s32[200,128]{1,0:T(8,128)S(1)} %get-tuple-element.24), channel_id=1, source_target_pairs={{0,6},{2,4},{4,2},{6,0},{8,14},{10,12},{12,10},{14,8},{16,22},{18,... | collective-permute-start | bytes 307208 | tf_op jit(solution)/shard_map/ppermute | solution.py:33
  27.2 2.2 %collective-permute-done.6.refs_0_ = s32[200,128]{1,0:T(8,128)S(1)} collective-permute-done((s32[200,128]{1,0:T(8,128)S(1)}, s32[200,128]{1,0:T(8,128)S(1)}, u32[]{:S(2)}, u32[]{:S(2)}) %collective-permute-start.6) | collective-permute-done | bytes 102432 | tf_op jit(solution)/shard_map/ppermute | solution.py:33
  29.5 0.2 collective-permute-done.7.refs_1_
  29.7 1.4 %collective-permute-done.8.refs_2_ = s32[200,128]{1,0:T(8,128)S(1)} collective-permute-done((s32[200,128]{1,0:T(8,128)S(1)}, s32[200,128]{1,0:T(8,128)S(1)}, u32[]{:S(2)}, u32[]{:S(2)}) %collective-permute-start.8) | collective-permute-done | bytes 102432 | tf_op jit(solution)/shard_map/ppermute | solution.py:33
  31.1 0.2 shard_map.49
  31.3 2.7 %collective-permute-start.10 = (s32[200,128]{1,0:T(8,128)S(1)}, s32[200,128]{1,0:T(8,128)S(1)}, u32[]{:S(2)}, u32[]{:S(2)}) collective-permute-start(s32[200,128]{1,0:T(8,128)S(1)} %shard_map.49), channel_id=1, source_target_pairs={{0,16},{2,18},{4,20},{6,22},{8,24},{10,26},{12,28},{14,30},{16,0},... | collective-permute-start | bytes 307208 | tf_op jit(solution)/shard_map/ppermute | solution.py:33
  33.9 2.9 %collective-permute-start.11 = (s32[200,128]{1,0:T(8,128)S(1)}, s32[200,128]{1,0:T(8,128)S(1)}, u32[]{:S(2)}, u32[]{:S(2)}) collective-permute-start(s32[200,128]{1,0:T(8,128)S(1)} %shard_map.49), channel_id=1, source_target_pairs={{0,24},{2,26},{4,28},{6,30},{8,16},{10,18},{12,20},{14,22},{16,8},... | collective-permute-start | bytes 307208 | tf_op jit(solution)/shard_map/ppermute | solution.py:33
  36.8 0.5 collective-permute-start.9
  37.3 4.9 %collective-permute-done.10.refs_4_ = s32[200,128]{1,0:T(8,128)S(1)} collective-permute-done((s32[200,128]{1,0:T(8,128)S(1)}, s32[200,128]{1,0:T(8,128)S(1)}, u32[]{:S(2)}, u32[]{:S(2)}) %collective-permute-start.10) | collective-permute-done | bytes 102432 | tf_op jit(solution)/shard_map/ppermute | solution.py:33
  42.2 0.7 %collective-permute-done.9.refs_3_ = s32[200,128]{1,0:T(8,128)S(1)} collective-permute-done((s32[200,128]{1,0:T(8,128)S(1)}, s32[200,128]{1,0:T(8,128)S(1)}, u32[]{:S(2)}, u32[]{:S(2)}) %collective-permute-start.9) | collective-permute-done | bytes 102432 | tf_op jit(solution)/shard_map/ppermute | solution.py:33
  42.9 1.0 %shard_map.50 = (f32[3,128,128]{2,1,0:T(8,128)S(1)}, s32[200,128]{1,0:T(8,128)S(1)}, s32[200,128]{1,0:T(8,128)S(1)}, s32[200,128]{1,0:T(8,128)S(1)}) custom-call(s32[5]{0:T(128)S(1)} %stack.23.where, f32[3,128,128]{2,1,0:T(8,128)S(1)} %get-tuple-element.21.mine, s32[200,128]{1,0:T(8,128)S(1)} %collective-permute-done.6.refs_0_, ...), custom_call_target="tpu_custom_call" | custom-call | tf_op jit(solution)/shard_map/pallas_call | solution.py:21
  43.9 1.0 %collective-permute-start.12 = (s32[200,128]{1,0:T(8,128)S(1)}, s32[200,128]{1,0:T(8,128)S(1)}, u32[]{:S(2)}, u32[]{:S(2)}) collective-permute-start(s32[200,128]{1,0:T(8,128)S(1)} %get-tuple-element.26), channel_id=1, source_target_pairs={{0,2},{2,0},{4,6},{6,4},{8,10},{10,8},{12,14},{14,12},{16,18},{18,... | collective-permute-start | bytes 307208 | tf_op jit(solution)/shard_map/ppermute | solution.py:33
  44.9 0.6 %collective-permute-start.13 = (s32[200,128]{1,0:T(8,128)S(1)}, s32[200,128]{1,0:T(8,128)S(1)}, u32[]{:S(2)}, u32[]{:S(2)}) collective-permute-start(s32[200,128]{1,0:T(8,128)S(1)} %get-tuple-element.27), channel_id=1, source_target_pairs={{0,4},{2,6},{4,0},{6,2},{8,12},{10,14},{12,8},{14,10},{16,20},{18,... | collective-permute-start | bytes 307208 | tf_op jit(solution)/shard_map/ppermute | solution.py:33
  45.5 2.0 %collective-permute-start.14 = (s32[200,128]{1,0:T(8,128)S(1)}, s32[200,128]{1,0:T(8,128)S(1)}, u32[]{:S(2)}, u32[]{:S(2)}) collective-permute-start(s32[200,128]{1,0:T(8,128)S(1)} %get-tuple-element.28), channel_id=1, source_target_pairs={{0,6},{2,4},{4,2},{6,0},{8,14},{10,12},{12,10},{14,8},{16,22},{18,... | collective-permute-start | bytes 307208 | tf_op jit(solution)/shard_map/ppermute | solution.py:33
  47.5 1.2 %collective-permute-done.12.refs_0_ = s32[200,128]{1,0:T(8,128)S(1)} collective-permute-done((s32[200,128]{1,0:T(8,128)S(1)}, s32[200,128]{1,0:T(8,128)S(1)}, u32[]{:S(2)}, u32[]{:S(2)}) %collective-permute-start.12) | collective-permute-done | bytes 102432 | tf_op jit(solution)/shard_map/ppermute | solution.py:33
  48.6 0.9 %collective-permute-done.13.refs_1_ = s32[200,128]{1,0:T(8,128)S(1)} collective-permute-done((s32[200,128]{1,0:T(8,128)S(1)}, s32[200,128]{1,0:T(8,128)S(1)}, u32[]{:S(2)}, u32[]{:S(2)}) %collective-permute-start.13) | collective-permute-done | bytes 102432 | tf_op jit(solution)/shard_map/ppermute | solution.py:33
  49.5 1.5 %collective-permute-done.14.refs_2_ = s32[200,128]{1,0:T(8,128)S(1)} collective-permute-done((s32[200,128]{1,0:T(8,128)S(1)}, s32[200,128]{1,0:T(8,128)S(1)}, u32[]{:S(2)}, u32[]{:S(2)}) %collective-permute-start.14) | collective-permute-done | bytes 102432 | tf_op jit(solution)/shard_map/ppermute | solution.py:33
  51.1 1.5 %shard_map.51 = f32[3,512,128]{2,1,0:T(8,128)} custom-call(s32[5]{0:T(128)S(1)} %stack.23.where, f32[3,512,128]{2,1,0:T(8,128)S(1)} %get-tuple-element.20.own, f32[3,128,128]{2,1,0:T(8,128)S(1)} %get-tuple-element.25.base, s32[200,128]{1,0:T(8,128)S(1)} %collective-permute-done.12.refs_0_, s32[200,128]{1,0:T(8,128)S(1)} %collective-permute-done.13.refs_1_, ...), custom_call_target="tpu_custom_call" | custom-call | tf_op jit(solution)/shard_map/pallas_call | solution.py:21
  (12 shorter events, 0.2 us)
Async XLA Ops:
  1.1 18.2 %collective-permute-start.3 = (bf16[2,1024,128]{2,1,0:T(8,128)(2,1)S(1)}, bf16[2,1024,128]{2,1,0:T(8,128)(2,1)S(1)}, u32[]{:S(2)}, u32[]{:S(2)}) collective-permute-start(bf16[2,1024,128]{2,1,0:T(8,128)(2,1)S(1)} %slice.3), channel_id=1, source_target_pairs={{0,30},{2,0},{4,2},{6,4},{8,6},{10,8},{12,10},{14,12},{16,14},{18,... | collective-permute-start | bytes 1572872 | tf_op jit(solution)/shard_map/ppermute | solution.py:187
  8.8 1.6 %copy-start = (bf16[1,1024,1024]{2,1,0:T(8,128)(2,1)S(1)}, bf16[1,1024,1024]{2,1,0:T(8,128)(2,1)}, u32[]{:S(2)}) copy-start(bf16[1,1024,1024]{2,1,0:T(8,128)(2,1)} %param.4) | copy-start | bytes 6291460
  10.4 1.2 %copy-start.1 = (bf16[4,1024,128]{2,1,0:T(8,128)(2,1)S(1)}, bf16[4,1024,128]{2,1,0:T(8,128)(2,1)}, u32[]{:S(2)}) copy-start(bf16[4,1024,128]{2,1,0:T(8,128)(2,1)} %own.1) | copy-start | bytes 3145732
  11.6 0.7 %copy-start.2 = (s32[1,128]{1,0:T(1,128)S(1)}, s32[1,128]{1,0:T(1,128)}, u32[]{:S(2)}) copy-start(s32[1,128]{1,0:T(1,128)} %refs_4_.1) | copy-start | bytes 1540
  13.2 6.6 %collective-permute-start.2 = (bf16[1024,384]{1,0:T(8,128)(2,1)S(1)}, bf16[1024,384]{1,0:T(8,128)(2,1)S(1)}, u32[]{:S(2)}, u32[]{:S(2)}) collective-permute-start(bf16[1024,384]{1,0:T(8,128)(2,1)S(1)} %get-tuple-element.19.refs_2_), channel_id=1, source_target_pairs={{0,1},{1,0},{2,3},{3,2},{4,5},{5,4},{6,7},{7,6},{8,9},{9,8},{10,11... | collective-permute-start | bytes 2359304 | tf_op jit(solution)/shard_map/ppermute | solution.py:33
  13.3 6.5 %collective-permute-start = (bf16[256,1024]{1,0:T(8,128)(2,1)S(1)}, bf16[256,1024]{1,0:T(8,128)(2,1)S(1)}, u32[]{:S(2)}, u32[]{:S(2)}) collective-permute-start(bf16[256,1024]{1,0:T(8,128)(2,1)S(1)} %get-tuple-element.17), channel_id=1, source_target_pairs={{0,1},{1,0},{2,3},{3,2},{4,5},{5,4},{6,7},{7,6},{8,9},{9,8},{10,11... | collective-permute-start | bytes 1572872 | tf_op jit(solution)/shard_map/ppermute | solution.py:33
  13.8 6.0 %collective-permute-start.1 = (bf16[256,1024]{1,0:T(8,128)(2,1)S(1)}, bf16[256,1024]{1,0:T(8,128)(2,1)S(1)}, u32[]{:S(2)}, u32[]{:S(2)}) collective-permute-start(bf16[256,1024]{1,0:T(8,128)(2,1)S(1)} %get-tuple-element.18), channel_id=1, source_target_pairs={{0,1},{1,0},{2,3},{3,2},{4,5},{5,4},{6,7},{7,6},{8,9},{9,8},{10,11... | collective-permute-start | bytes 1572872 | tf_op jit(solution)/shard_map/ppermute | solution.py:33
  19.2 2.3 %collective-permute-start.4 = (bf16[2,1024,128]{2,1,0:T(8,128)(2,1)S(1)}, bf16[2,1024,128]{2,1,0:T(8,128)(2,1)S(1)}, u32[]{:S(2)}, u32[]{:S(2)}) collective-permute-start(bf16[2,1024,128]{2,1,0:T(8,128)(2,1)S(1)} %collective-permute-done.3.refs_2_), channel_id=1, source_target_pairs={{0,1},{1,0},{2,3},{3,2},{4,5},{5,4},{6,7},{7,6},{8,9},{9,8},{10,11... | collective-permute-start | bytes 1572872 | tf_op jit(solution)/shard_map/ppermute | solution.py:33
  19.3 2.3 %collective-permute-start.5 = (s32[1,128]{1,0:T(1,128)S(1)}, s32[1,128]{1,0:T(1,128)S(1)}, u32[]{:S(2)}, u32[]{:S(2)}) collective-permute-start(s32[1,128]{1,0:T(1,128)S(1)} %copy-done.2), channel_id=1, source_target_pairs={{0,1},{1,0},{2,3},{3,2},{4,5},{5,4},{6,7},{7,6},{8,9},{9,8},{10,11... | collective-permute-start | bytes 1544 | tf_op jit(solution)/shard_map/ppermute | solution.py:33
  23.7 5.8 %collective-permute-start.6 = (s32[200,128]{1,0:T(8,128)S(1)}, s32[200,128]{1,0:T(8,128)S(1)}, u32[]{:S(2)}, u32[]{:S(2)}) collective-permute-start(s32[200,128]{1,0:T(8,128)S(1)} %get-tuple-element.22), channel_id=1, source_target_pairs={{0,2},{2,0},{4,6},{6,4},{8,10},{10,8},{12,14},{14,12},{16,18},{18,... | collective-permute-start | bytes 307208 | tf_op jit(solution)/shard_map/ppermute | solution.py:33
  23.8 6.0 %collective-permute-start.7 = (s32[200,128]{1,0:T(8,128)S(1)}, s32[200,128]{1,0:T(8,128)S(1)}, u32[]{:S(2)}, u32[]{:S(2)}) collective-permute-start(s32[200,128]{1,0:T(8,128)S(1)} %get-tuple-element.23), channel_id=1, source_target_pairs={{0,4},{2,6},{4,0},{6,2},{8,12},{10,14},{12,8},{14,10},{16,20},{18,... | collective-permute-start | bytes 307208 | tf_op jit(solution)/shard_map/ppermute | solution.py:33
  25.5 5.6 %collective-permute-start.8 = (s32[200,128]{1,0:T(8,128)S(1)}, s32[200,128]{1,0:T(8,128)S(1)}, u32[]{:S(2)}, u32[]{:S(2)}) collective-permute-start(s32[200,128]{1,0:T(8,128)S(1)} %get-tuple-element.24), channel_id=1, source_target_pairs={{0,6},{2,4},{4,2},{6,0},{8,14},{10,12},{12,10},{14,8},{16,22},{18,... | collective-permute-start | bytes 307208 | tf_op jit(solution)/shard_map/ppermute | solution.py:33
  31.3 10.9 %collective-permute-start.10 = (s32[200,128]{1,0:T(8,128)S(1)}, s32[200,128]{1,0:T(8,128)S(1)}, u32[]{:S(2)}, u32[]{:S(2)}) collective-permute-start(s32[200,128]{1,0:T(8,128)S(1)} %shard_map.49), channel_id=1, source_target_pairs={{0,16},{2,18},{4,20},{6,22},{8,24},{10,26},{12,28},{14,30},{16,0},... | collective-permute-start | bytes 307208 | tf_op jit(solution)/shard_map/ppermute | solution.py:33
  33.9 8.3 %collective-permute-start.11 = (s32[200,128]{1,0:T(8,128)S(1)}, s32[200,128]{1,0:T(8,128)S(1)}, u32[]{:S(2)}, u32[]{:S(2)}) collective-permute-start(s32[200,128]{1,0:T(8,128)S(1)} %shard_map.49), channel_id=1, source_target_pairs={{0,24},{2,26},{4,28},{6,30},{8,16},{10,18},{12,20},{14,22},{16,8},... | collective-permute-start | bytes 307208 | tf_op jit(solution)/shard_map/ppermute | solution.py:33
  36.8 6.1 %collective-permute-start.9 = (s32[200,128]{1,0:T(8,128)S(1)}, s32[200,128]{1,0:T(8,128)S(1)}, u32[]{:S(2)}, u32[]{:S(2)}) collective-permute-start(s32[200,128]{1,0:T(8,128)S(1)} %shard_map.49), channel_id=1, source_target_pairs={{0,8},{2,10},{4,12},{6,14},{8,0},{10,2},{12,4},{14,6},{16,24},{18,... | collective-permute-start | bytes 307208 | tf_op jit(solution)/shard_map/ppermute | solution.py:33
  43.9 4.7 %collective-permute-start.12 = (s32[200,128]{1,0:T(8,128)S(1)}, s32[200,128]{1,0:T(8,128)S(1)}, u32[]{:S(2)}, u32[]{:S(2)}) collective-permute-start(s32[200,128]{1,0:T(8,128)S(1)} %get-tuple-element.26), channel_id=1, source_target_pairs={{0,2},{2,0},{4,6},{6,4},{8,10},{10,8},{12,14},{14,12},{16,18},{18,... | collective-permute-start | bytes 307208 | tf_op jit(solution)/shard_map/ppermute | solution.py:33
  44.9 4.7 %collective-permute-start.13 = (s32[200,128]{1,0:T(8,128)S(1)}, s32[200,128]{1,0:T(8,128)S(1)}, u32[]{:S(2)}, u32[]{:S(2)}) collective-permute-start(s32[200,128]{1,0:T(8,128)S(1)} %get-tuple-element.27), channel_id=1, source_target_pairs={{0,4},{2,6},{4,0},{6,2},{8,12},{10,14},{12,8},{14,10},{16,20},{18,... | collective-permute-start | bytes 307208 | tf_op jit(solution)/shard_map/ppermute | solution.py:33
  45.5 5.6 %collective-permute-start.14 = (s32[200,128]{1,0:T(8,128)S(1)}, s32[200,128]{1,0:T(8,128)S(1)}, u32[]{:S(2)}, u32[]{:S(2)}) collective-permute-start(s32[200,128]{1,0:T(8,128)S(1)} %get-tuple-element.28), channel_id=1, source_target_pairs={{0,6},{2,4},{4,2},{6,0},{8,14},{10,12},{12,10},{14,8},{16,22},{18,... | collective-permute-start | bytes 307208 | tf_op jit(solution)/shard_map/ppermute | solution.py:33

commit v3 on v2

--- a/solution.py
+++ b/solution.py
@@ -10,6 +10,8 @@
 TICKS = 3
 PARTS = 2
 INNER = 4
+PADS = {2: 16, 3: 8}
+MASKS = tuple(range(INNER - 1, 0, -1))
 VMEM = pl.BlockSpec(memory_space=pltpu.VMEM)
 SMEM = pl.BlockSpec(memory_space=pltpu.SMEM)
 HBM = pl.BlockSpec(memory_space=pl.ANY)
@@ -47,7 +49,7 @@
 
 
 def unpack(ref, half):
-    ticks = (ref.shape[0] - 8) // half
+    ticks = TICKS
     unit = jnp.exp2(ref[ticks * half : ticks * half + 8, :].astype(jnp.float32) - 15.0)
     values = []
     for t in range(ticks):
@@ -76,39 +78,56 @@
         out[...] = taps[pl.ds(pl.multiple_of(first, rows), rows), :]
 
 
-def base_kernel(n_col, where, taps, *refs):
-    others, windows, out = refs[: (n_col - 1) * PARTS], refs[(n_col - 1) * PARTS : -1], refs[-1]
-    rows, width = out.shape[1], out.shape[2]
-    mine = taps[pl.ds(pl.multiple_of(where[0] * rows, rows), rows), :]
-    total = jnp.dot(mine, windows[0][...], preferred_element_type=jnp.float32)
-    for i, window in enumerate(windows[1:]):
-        other = jnp.concatenate([ref[...] for ref in others[i * PARTS : (i + 1) * PARTS]], axis=0)
-        total = total + jnp.dot(other, window[...], preferred_element_type=jnp.float32)
+def ordered(newer, slots):
+    chosen = chooser(slots)
+    parts = [jnp.dot(newer[j], chosen, preferred_element_type=jnp.float32) for j in range(TICKS - 1)]
+    return jnp.concatenate([part.astype(jnp.bfloat16) for part in parts], axis=1)
+
+
+def used(where, offset, t, j):
+    return (offset[0] + t == where[1] + j) & (where[2] == 0)
+
+
+def base_kernel(n_col, where, offset, taps, newer, slots, *refs):
+    cut = (n_col - 1) * PARTS
+    others, windows, out = refs[:cut], refs[cut:-1], refs[-1]
+    rows, width = out.shape[1:]
+    late = ordered(newer, slots)
+    ticks = []
     for t in range(TICKS):
-        out[t] = total[:, t * width : (t + 1) * width]
-
-
-def late_kernel(n_col, where, offset, taps, base, *refs):
+        value = windows[0][:, t * width : (t + 1) * width]
+        for j in range(t):
+            value = jnp.where(used(where, offset, t, j), late[:, j * width : (j + 1) * width], value)
+        ticks.append(value)
+    right = jnp.concatenate(ticks, axis=1)
+    part = rows // PARTS
+    for p in range(PARTS):
+        first = pl.multiple_of(where[0] * rows + p * part, part)
+        total = jnp.dot(taps[pl.ds(first, part), :], right, preferred_element_type=jnp.float32)
+        for i, window in enumerate(windows[1:]):
+            total = total + jnp.dot(others[i * PARTS + p][...], window[...], preferred_element_type=jnp.float32)
+        for t in range(TICKS):
+            out[t, p * part : (p + 1) * part, :] = total[:, t * width : (t + 1) * width]
+
+
+def late_kernel(n_col, where, offset, base, *refs):
     cut = (n_col - 1) * PARTS
-    others, newer, slots = refs[:cut], refs[cut : cut + n_col], refs[cut + n_col : cut + 2 * n_col]
-    own, mine, *sends = refs[cut + 2 * n_col :]
+    others, newer, slots = refs[:cut], refs[cut : cut + n_col - 1], refs[cut + n_col - 1 : cut + 2 * n_col - 2]
+    own, mine, *sends = refs[cut + 2 * n_col - 2 :]
     _, rows, width = base.shape
-    local = taps[pl.ds(pl.multiple_of(where[0] * rows, rows), rows), :]
-    total = 0.0
-    for i in range(n_col):
-        chosen = chooser(slots[i])
-        parts = [jnp.dot(newer[i][j], chosen, preferred_element_type=jnp.float32) for j in range(TICKS - 1)]
-        rhs = jnp.concatenate([part.astype(jnp.bfloat16) for part in parts], axis=1)
-        lhs = jnp.concatenate([ref[...] for ref in others[(i - 1) * PARTS : i * PARTS]], axis=0) if i else local
-        total = total + jnp.dot(lhs, rhs, preferred_element_type=jnp.float32)
-    for t in range(TICKS):
-        value = base[t]
-        for j in range(t):
-            used = (offset[0] + t == where[1] + j) & (where[2] == 0)
-            value = value + jnp.where(used, total[:, j * width : (j + 1) * width], 0.0)
-        own[t] = value
+    right = [ordered(*pair) for pair in zip(newer, slots)]
+    part = rows // PARTS
+    for p in range(PARTS):
+        total = jnp.dot(others[p][...], right[0], preferred_element_type=jnp.float32)
+        for i in range(1, n_col - 1):
+            total = total + jnp.dot(others[i * PARTS + p][...], right[i], preferred_element_type=jnp.float32)
+        for t in range(TICKS):
+            value = base[t, p * part : (p + 1) * part, :]
+            for j in range(t):
+                value = value + jnp.where(used(where, offset, t, j), total[:, j * width : (j + 1) * width], 0.0)
+            own[t, p * part : (p + 1) * part, :] = value
     piece = rows // INNER
-    for k, out in enumerate((mine, *sends)):
+    for k, out in zip((0, *MASKS), (mine, *sends)):
         first = pl.multiple_of((where[3] ^ k) * piece, piece)
         value = own[:, pl.ds(first, piece), :]
         if k:
@@ -118,38 +137,51 @@
 
 
 def total_kernel(mine, *refs):
-    received, out = refs[:-1], refs[-1]
+    received, outs = refs[: INNER - 1], refs[INNER - 1 :]
     half = mine.shape[1] // 2
     total = mine[...]
     for ref in received:
         total = total + unpack(ref, half)
-    pack(total, out)
-
-
-def prefix_kernel(n_outer, where, mine, *refs):
-    received, totals, (base, *sends) = refs[: INNER - 1], refs[INNER - 1 : INNER + n_outer - 2], refs[INNER + n_outer - 2 :]
+    size = TICKS * half + 8
+    for i, out in enumerate(outs):
+        if i:
+            out[:size, :] = outs[0][:size, :]
+        else:
+            pack(total, out)
+        if out.shape[0] > size:
+            out[size:, :] = jnp.zeros((out.shape[0] - size, out.shape[1]), jnp.int32)
+
+
+def inner_kernel(where, mine, *refs):
+    received, outs = refs[: INNER - 1], refs[INNER - 1 :]
     half = mine.shape[1] // 2
-    place, group = where[3], where[4]
-    earlier = jnp.zeros(mine.shape, jnp.float32)
+    place = where[3]
+    terms = [mine[...]] + [unpack(ref, half) for ref in received]
+    for k, out in zip((0, *MASKS), outs):
+        value = jnp.zeros(mine.shape, jnp.float32)
+        for m, term in zip((0, *MASKS), terms):
+            if m != k:
+                value = value + jnp.where((place ^ m) < (place ^ k), term, 0.0)
+        out[...] = value
+
+
+def prefix_kernel(where, *refs):
+    inner, totals, (base, *sends) = refs[:INNER], refs[INNER:-INNER], refs[-INNER:]
+    half = base.shape[1] // 2
+    group = where[4]
+    earlier = jnp.zeros(base.shape, jnp.float32)
     for k, ref in enumerate(totals, 1):
         earlier = earlier + jnp.where((group ^ k) < group, unpack(ref, half), 0.0)
-    terms = [mine[...]] + [unpack(ref, half) for ref in received]
-    for k, out in enumerate((base, *sends)):
-        value = earlier
-        for m, term in enumerate(terms):
-            if m != k:
-                value = value + jnp.where((place ^ m) < (place ^ k), term, 0.0)
-        if k:
-            pack(value, out)
-        else:
-            out[...] = value
+    base[...] = inner[0][...] + earlier
+    for ref, out in zip(inner[1:], sends):
+        pack(ref[...] + earlier, out)
 
 
 def finish_kernel(where, own, base, *refs):
     received, (out, ready, sems) = refs[:-3], refs[-3:]
     piece = base.shape[1]
     copies = []
-    for k, ref in enumerate((base, *received)):
+    for k, ref in zip((0, *MASKS), (base, *received)):
         first = pl.multiple_of((where[3] ^ k) * piece, piece)
         older = unpack(ref, piece // 2) if k else ref[...]
         ready[k] = own[:, pl.ds(first, piece), :] + older
@@ -160,9 +192,7 @@
 
 
 def among_members(values):
-    order = range(len(values), 0, -1)
-    arrived = {k: swapped(values[k - 1], "lag", k) for k in order}
-    return [arrived[k] for k in range(1, len(values) + 1)]
+    return [swapped(value, "lag", k) for k, value in zip(MASKS, values)]
 
 
 def local(tap_matrices, density_history, offsets, column_slots):
@@ -192,22 +222,22 @@
     )
     others = [swapped(value, "col", 1 + i // PARTS) for i, value in enumerate(tap_sends)]
     windows = [window] + [swapped(window, "col", k) for k in range(1, n_col)]
-    [base] = call(functools.partial(base_kernel, n_col), [f32(rows)], [where, taps, *others, *windows])
-    newer = [newer] + [swapped(newer, "col", k) for k in range(1, n_col)]
-    slots = [column_slots] + [swapped(column_slots, "col", k) for k in range(1, n_col)]
+    [base] = call(
+        functools.partial(base_kernel, n_col), [f32(rows)], [where, offsets, taps, newer, column_slots, *others, *windows]
+    )
+    newer = [swapped(newer, "col", k) for k in range(1, n_col)]
+    slots = [swapped(column_slots, "col", k) for k in range(1, n_col)]
     own, mine, *sends = call(
         functools.partial(late_kernel, n_col),
         [f32(rows), f32(piece)] + [packed] * (INNER - 1),
-        [where, offsets, taps, base, *others, *newer, *slots],
+        [where, offsets, base, *others, *newer, *slots],
     )
     received = among_members(sends)
-    [total] = call(total_kernel, [packed], [mine, *received])
-    totals = [swapped(total, "lag", k * INNER) for k in range(1, n_outer)]
-    older, *sends = call(
-        functools.partial(prefix_kernel, n_outer),
-        [f32(piece)] + [packed] * (INNER - 1),
-        [where, mine, *received, *totals],
-    )
+    far = [jax.ShapeDtypeStruct((packed.shape[0] + PADS.get(k, 0), width), jnp.int32) for k in range(1, n_outer)]
+    sums = call(total_kernel, far, [mine, *received])
+    totals = [swapped(total, "lag", k * INNER) for k, total in enumerate(sums, 1)]
+    inner = call(inner_kernel, [f32(piece)] * INNER, [where, mine, *received])
+    older, *sends = call(prefix_kernel, [f32(piece)] + [packed] * (INNER - 1), [where, *inner, *totals])
     received = among_members(sends)
     [history_sum] = call(
         finish_kernel,

time: 52.8 us -> 52.2 us (0.989)
  starting transfers between devices: 21.3 us -> 19.9 us
  waiting for transfers between devices: 18.5 us -> 19.4 us
    ppermute x14, starting transfers between devices: 14.3 us -> 12.9 us  [swapped(): return lax.ppermute(value, axis, [(i, i ^ mask) for i in range(count)])]
    ppermute x14, waiting for transfers between devices: 13.1 us -> 14 us  [swapped(): return lax.ppermute(value, axis, [(i, i ^ mask) for i in range(count)])]
    pallas_call x6 -> x7, Pallas kernels: 7.43 us -> 7.38 us  [call(): pl.pallas_call(kernel, out_shape=out_shape, in_specs=[SMEM if a.ndim == 1...]
  transfers between devices with their start and end apart: 15 -> 15, of which waited for: 9 -> 6; matrix products, arithmetic and copies ran while one was open for 0% -> 0% of each run, Pallas kernels for 5% -> 7%
where the time goes in v3:
time: 52.2 us; the launch traced here: 52 us
  starting transfers between devices  19.9 us (38%)
  waiting for transfers between devices  19.4 us (37%)
  Pallas kernels  7.38 us (14%)
  local copies, waits for them, and re-layouts  4.63 us (9%)
  between operations  0.74 us (1%)
    ppermute x14, waiting for transfers between devices, swapped(): return lax.ppermute(value, axis, [(i, i ^ mask) for i in range(count)])  14 us
    ppermute x14, starting transfers between devices, swapped(): return lax.ppermute(value, axis, [(i, i ^ mask) for i in range(count)])  12.9 us
    pallas_call x7, Pallas kernels, call(): pl.pallas_call(kernel, out_shape=out_shape, in_specs=[SMEM if a.ndim == 1...  7.38 us
    ppermute x1, starting transfers between devices, local(): lax.ppermute(density_history[:TICKS - 1], 'lag', [(i, (i - 1) % n_lag) fo...  6.98 us
    ppermute x1, waiting for transfers between devices, local(): lax.ppermute(density_history[:TICKS - 1], 'lag', [(i, (i - 1) % n_lag) fo...  5.38 us
    unnamed x6, local copies, waits for them, and re-layouts  3.47 us
    slice x1, local copies, waits for them, and re-layouts, local(): density_history[:TICKS - 1]  1.08 us
  transfers between devices with their start and end apart: 15, of which 6 were waited for; matrix products, arithmetic and copies ran while one was open for 0% of the time, Pallas kernels for 7%

profile of v3, /device:TPU:0, one launch (start us, length us, event | category | flops | bytes accessed | tf_op | source)
XLA Modules:
  0.0 52.0 jit_solution(7899262705966812073)
XLA Ops:
  0.0 1.1 %slice.3 = bf16[2,1024,128]{2,1,0:T(8,128)(2,1)S(1)} slice(bf16[4,1024,128]{2,1,0:T(8,128)(2,1)} %own.1), slice={[0:2], [0:1024], [0:128]} | slice | bytes 1048576 | tf_op jit(solution)/shard_map/slice | solution.py:217
  1.1 7.0 %collective-permute-start = (bf16[2,1024,128]{2,1,0:T(8,128)(2,1)S(1)}, bf16[2,1024,128]{2,1,0:T(8,128)(2,1)S(1)}, u32[]{:S(2)}, u32[]{:S(2)}) collective-permute-start(bf16[2,1024,128]{2,1,0:T(8,128)(2,1)S(1)} %slice.3), channel_id=1, source_target_pairs={{0,30},{2,0},{4,2},{6,4},{8,6},{10,8},{12,10},{14,12},{16,14},{18,... | collective-permute-start | bytes 1572872 | tf_op jit(solution)/shard_map/ppermute | solution.py:217
  8.7 0.1 stack.23.where
  8.8 1.6 %copy-done = bf16[1,1024,1024]{2,1,0:T(8,128)(2,1)S(1)} copy-done((bf16[1,1024,1024]{2,1,0:T(8,128)(2,1)S(1)}, bf16[1,1024,1024]{2,1,0:T(8,128)(2,1)}, u32[]{:S(2)}) %copy-start) | copy-done | bytes 2097176
  10.4 1.2 %copy-done.1 = bf16[4,1024,128]{2,1,0:T(8,128)(2,1)S(1)} copy-done((bf16[4,1024,128]{2,1,0:T(8,128)(2,1)S(1)}, bf16[4,1024,128]{2,1,0:T(8,128)(2,1)}, u32[]{:S(2)}) %copy-start.1) | copy-done | bytes 1048600
  11.6 0.7 %copy-done.2 = s32[1,128]{1,0:T(1,128)S(1)} copy-done((s32[1,128]{1,0:T(1,128)S(1)}, s32[1,128]{1,0:T(1,128)}, u32[]{:S(2)}) %copy-start.2) | copy-done | bytes 536
  12.3 0.9 %shard_map.46 = (bf16[1024,384]{1,0:T(8,128)(2,1)S(1)}, bf16[256,1024]{1,0:T(8,128)(2,1)S(1)}, bf16[256,1024]{1,0:T(8,128)(2,1)S(1)}) custom-call(s32[5]{0:T(128)S(1)} %stack.23.where, s32[1]{0:T(128)S(6)} %copy.5.offset, bf16[1024,1024]{1,0:T(8,128)(2,1)S(1)} %bitcast.8, bf16[4,1024,128]{2,1,0:T(8,128)(2,1)S(1)} %copy-done.1, s32[1,128]{1,0:T(1,128)S(1)} %copy-done.2), custom_call_target="tpu_custom_call" | custom-call | tf_op jit(solution)/shard_map/pallas_call | solution.py:23
  13.2 0.1 collective-permute-start.3
  13.3 0.5 collective-permute-start.1
  13.8 0.1 collective-permute-start.2
  13.9 5.4 %collective-permute-done.newer = bf16[2,1024,128]{2,1,0:T(8,128)(2,1)S(1)} collective-permute-done((bf16[2,1024,128]{2,1,0:T(8,128)(2,1)S(1)}, bf16[2,1024,128]{2,1,0:T(8,128)(2,1)S(1)}, u32[]{:S(2)}, u32[]{:S(2)}) %collective-permute-start) | collective-permute-done | bytes 524320 | tf_op jit(solution)/shard_map/ppermute | solution.py:217
  19.3 0.5 collective-permute-start.5
  19.8 0.0 collective-permute-done.1.refs_0_
  19.8 1.9 %shard_map.47.base = f32[3,512,128]{2,1,0:T(8,128)S(1)} custom-call(s32[5]{0:T(128)S(1)} %stack.23.where, s32[1]{0:T(128)S(6)} %copy.5.offset, bf16[1024,1024]{1,0:T(8,128)(2,1)S(1)} %bitcast.9, bf16[2,1024,128]{2,1,0:T(8,128)(2,1)S(1)} %collective-permute-done.newer, s32[1,128]{1,0:T(1,128)S(1)} %copy-done.2, ...), custom_call_target="tpu_custom_call" | custom-call | tf_op jit(solution)/shard_map/pallas_call | solution.py:23
  21.7 1.3 %shard_map.48 = (f32[3,512,128]{2,1,0:T(8,128)S(1)}, f32[3,128,128]{2,1,0:T(8,128)S(1)}, s32[200,128]{1,0:T(8,128)S(1)}, s32[200,128]{1,0:T(8,128)S(1)}, s32[200,128]{1,0:T(8,128)S(1)}) custom-call(s32[5]{0:T(128)S(1)} %stack.23.where, s32[1]{0:T(128)S(6)} %copy.5.offset, f32[3,512,128]{2,1,0:T(8,128)S(1)} %shard_map.47.base, ...), custom_call_target="tpu_custom_call" | custom-call | tf_op jit(solution)/shard_map/pallas_call | solution.py:23
  23.1 1.3 %collective-permute-start.6 = (s32[200,128]{1,0:T(8,128)S(1)}, s32[200,128]{1,0:T(8,128)S(1)}, u32[]{:S(2)}, u32[]{:S(2)}) collective-permute-start(s32[200,128]{1,0:T(8,128)S(1)} %get-tuple-element.29), channel_id=1, source_target_pairs={{0,6},{2,4},{4,2},{6,0},{8,14},{10,12},{12,10},{14,8},{16,22},{18,... | collective-permute-start | bytes 307208 | tf_op jit(solution)/shard_map/ppermute | solution.py:35
  24.4 2.2 %collective-permute-start.8 = (s32[200,128]{1,0:T(8,128)S(1)}, s32[200,128]{1,0:T(8,128)S(1)}, u32[]{:S(2)}, u32[]{:S(2)}) collective-permute-start(s32[200,128]{1,0:T(8,128)S(1)} %get-tuple-element.31), channel_id=1, source_target_pairs={{0,2},{2,0},{4,6},{6,4},{8,10},{10,8},{12,14},{14,12},{16,18},{18,... | collective-permute-start | bytes 307208 | tf_op jit(solution)/shard_map/ppermute | solution.py:35
  26.6 3.2 %collective-permute-done.6.refs_0_ = s32[200,128]{1,0:T(8,128)S(1)} collective-permute-done((s32[200,128]{1,0:T(8,128)S(1)}, s32[200,128]{1,0:T(8,128)S(1)}, u32[]{:S(2)}, u32[]{:S(2)}) %collective-permute-start.6) | collective-permute-done | bytes 102432 | tf_op jit(solution)/shard_map/ppermute | solution.py:35
  29.8 1.2 %collective-permute-done.7.refs_1_ = s32[200,128]{1,0:T(8,128)S(1)} collective-permute-done((s32[200,128]{1,0:T(8,128)S(1)}, s32[200,128]{1,0:T(8,128)S(1)}, u32[]{:S(2)}, u32[]{:S(2)}) %collective-permute-start.7) | collective-permute-done | bytes 102432 | tf_op jit(solution)/shard_map/ppermute | solution.py:35
  31.0 0.2 shard_map.50
  31.2 1.3 %collective-permute-start.10 = (s32[216,128]{1,0:T(8,128)S(1)}, s32[216,128]{1,0:T(8,128)S(1)}, u32[]{:S(2)}, u32[]{:S(2)}) collective-permute-start(s32[216,128]{1,0:T(8,128)S(1)} %get-tuple-element.37), channel_id=1, source_target_pairs={{0,16},{2,18},{4,20},{6,22},{8,24},{10,26},{12,28},{14,30},{16,0},... | collective-permute-start | bytes 331784 | tf_op jit(solution)/shard_map/ppermute | solution.py:35
  32.4 2.9 %collective-permute-start.11 = (s32[208,128]{1,0:T(8,128)S(1)}, s32[208,128]{1,0:T(8,128)S(1)}, u32[]{:S(2)}, u32[]{:S(2)}) collective-permute-start(s32[208,128]{1,0:T(8,128)S(1)} %get-tuple-element.38), channel_id=1, source_target_pairs={{0,24},{2,26},{4,28},{6,30},{8,16},{10,18},{12,20},{14,22},{16,8},... | collective-permute-start | bytes 319496 | tf_op jit(solution)/shard_map/ppermute | solution.py:35
  35.3 0.5 collective-permute-start.9
  35.8 0.8 %shard_map.49 = (f32[3,128,128]{2,1,0:T(8,128)S(1)}, f32[3,128,128]{2,1,0:T(8,128)S(1)}, f32[3,128,128]{2,1,0:T(8,128)S(1)}, f32[3,128,128]{2,1,0:T(8,128)S(1)}) custom-call(s32[5]{0:T(128)S(1)} %stack.23.where, f32[3,128,128]{2,1,0:T(8,128)S(1)} %get-tuple-element.28.mine, s32[200,128]{1,0:T(8,128)S(1)} %collective-permute-done.6.refs_0_, ...), custom_call_target="tpu_custom_call" | custom-call | tf_op jit(solution)/shard_map/pallas_call | solution.py:23
  36.6 6.4 %collective-permute-done.9.refs_4_ = s32[200,128]{1,0:T(8,128)S(1)} collective-permute-done((s32[200,128]{1,0:T(8,128)S(1)}, s32[200,128]{1,0:T(8,128)S(1)}, u32[]{:S(2)}, u32[]{:S(2)}) %collective-permute-start.9) | collective-permute-done | bytes 102432 | tf_op jit(solution)/shard_map/ppermute | solution.py:35
  43.0 0.8 %shard_map.51 = (f32[3,128,128]{2,1,0:T(8,128)S(1)}, s32[200,128]{1,0:T(8,128)S(1)}, s32[200,128]{1,0:T(8,128)S(1)}, s32[200,128]{1,0:T(8,128)S(1)}) custom-call(s32[5]{0:T(128)S(1)} %stack.23.where, f32[3,128,128]{2,1,0:T(8,128)S(1)} %get-tuple-element.32.refs_0_, f32[3,128,128]{2,1,0:T(8,128)S(1)} %get-tuple-element.33.refs_1_, ...), custom_call_target="tpu_custom_call" | custom-call | tf_op jit(solution)/shard_map/pallas_call | solution.py:23
  43.8 1.1 %collective-permute-start.12 = (s32[200,128]{1,0:T(8,128)S(1)}, s32[200,128]{1,0:T(8,128)S(1)}, u32[]{:S(2)}, u32[]{:S(2)}) collective-permute-start(s32[200,128]{1,0:T(8,128)S(1)} %get-tuple-element.40), channel_id=1, source_target_pairs={{0,6},{2,4},{4,2},{6,0},{8,14},{10,12},{12,10},{14,8},{16,22},{18,... | collective-permute-start | bytes 307208 | tf_op jit(solution)/shard_map/ppermute | solution.py:35
  44.9 0.3 collective-permute-start.13
  45.3 2.1 %collective-permute-start.14 = (s32[200,128]{1,0:T(8,128)S(1)}, s32[200,128]{1,0:T(8,128)S(1)}, u32[]{:S(2)}, u32[]{:S(2)}) collective-permute-start(s32[200,128]{1,0:T(8,128)S(1)} %get-tuple-element.42), channel_id=1, source_target_pairs={{0,2},{2,0},{4,6},{6,4},{8,10},{10,8},{12,14},{14,12},{16,18},{18,... | collective-permute-start | bytes 307208 | tf_op jit(solution)/shard_map/ppermute | solution.py:35
  47.4 2.2 %collective-permute-done.12.refs_0_ = s32[200,128]{1,0:T(8,128)S(1)} collective-permute-done((s32[200,128]{1,0:T(8,128)S(1)}, s32[200,128]{1,0:T(8,128)S(1)}, u32[]{:S(2)}, u32[]{:S(2)}) %collective-permute-start.12) | collective-permute-done | bytes 102432 | tf_op jit(solution)/shard_map/ppermute | solution.py:35
  49.5 1.0 %collective-permute-done.13.refs_1_ = s32[200,128]{1,0:T(8,128)S(1)} collective-permute-done((s32[200,128]{1,0:T(8,128)S(1)}, s32[200,128]{1,0:T(8,128)S(1)}, u32[]{:S(2)}, u32[]{:S(2)}) %collective-permute-start.13) | collective-permute-done | bytes 102432 | tf_op jit(solution)/shard_map/ppermute | solution.py:35
  50.5 1.5 %shard_map.52 = f32[3,512,128]{2,1,0:T(8,128)} custom-call(s32[5]{0:T(128)S(1)} %stack.23.where, f32[3,512,128]{2,1,0:T(8,128)S(1)} %get-tuple-element.27.own, f32[3,128,128]{2,1,0:T(8,128)S(1)} %get-tuple-element.39.base, s32[200,128]{1,0:T(8,128)S(1)} %collective-permute-done.12.refs_0_, s32[200,128]{1,0:T(8,128)S(1)} %collective-permute-done.13.refs_1_, ...), custom_call_target="tpu_custom_call" | custom-call | tf_op jit(solution)/shard_map/pallas_call | solution.py:23
  (13 shorter events, 0.0 us)
Async XLA Ops:
  1.1 18.2 %collective-permute-start = (bf16[2,1024,128]{2,1,0:T(8,128)(2,1)S(1)}, bf16[2,1024,128]{2,1,0:T(8,128)(2,1)S(1)}, u32[]{:S(2)}, u32[]{:S(2)}) collective-permute-start(bf16[2,1024,128]{2,1,0:T(8,128)(2,1)S(1)} %slice.3), channel_id=1, source_target_pairs={{0,30},{2,0},{4,2},{6,4},{8,6},{10,8},{12,10},{14,12},{16,14},{18,... | collective-permute-start | bytes 1572872 | tf_op jit(solution)/shard_map/ppermute | solution.py:217
  8.8 1.6 %copy-start = (bf16[1,1024,1024]{2,1,0:T(8,128)(2,1)S(1)}, bf16[1,1024,1024]{2,1,0:T(8,128)(2,1)}, u32[]{:S(2)}) copy-start(bf16[1,1024,1024]{2,1,0:T(8,128)(2,1)} %param.4) | copy-start | bytes 6291460
  10.4 1.2 %copy-start.1 = (bf16[4,1024,128]{2,1,0:T(8,128)(2,1)S(1)}, bf16[4,1024,128]{2,1,0:T(8,128)(2,1)}, u32[]{:S(2)}) copy-start(bf16[4,1024,128]{2,1,0:T(8,128)(2,1)} %own.1) | copy-start | bytes 3145732
  11.6 0.7 %copy-start.2 = (s32[1,128]{1,0:T(1,128)S(1)}, s32[1,128]{1,0:T(1,128)}, u32[]{:S(2)}) copy-start(s32[1,128]{1,0:T(1,128)} %slots.3) | copy-start | bytes 1540
  13.2 6.6 %collective-permute-start.3 = (bf16[1024,384]{1,0:T(8,128)(2,1)S(1)}, bf16[1024,384]{1,0:T(8,128)(2,1)S(1)}, u32[]{:S(2)}, u32[]{:S(2)}) collective-permute-start(bf16[1024,384]{1,0:T(8,128)(2,1)S(1)} %get-tuple-element.26.refs_2_), channel_id=1, source_target_pairs={{0,1},{1,0},{2,3},{3,2},{4,5},{5,4},{6,7},{7,6},{8,9},{9,8},{10,11... | collective-permute-start | bytes 2359304 | tf_op jit(solution)/shard_map/ppermute | solution.py:35
  13.3 6.5 %collective-permute-start.1 = (bf16[256,1024]{1,0:T(8,128)(2,1)S(1)}, bf16[256,1024]{1,0:T(8,128)(2,1)S(1)}, u32[]{:S(2)}, u32[]{:S(2)}) collective-permute-start(bf16[256,1024]{1,0:T(8,128)(2,1)S(1)} %get-tuple-element.24), channel_id=1, source_target_pairs={{0,1},{1,0},{2,3},{3,2},{4,5},{5,4},{6,7},{7,6},{8,9},{9,8},{10,11... | collective-permute-start | bytes 1572872 | tf_op jit(solution)/shard_map/ppermute | solution.py:35
  13.8 6.0 %collective-permute-start.2 = (bf16[256,1024]{1,0:T(8,128)(2,1)S(1)}, bf16[256,1024]{1,0:T(8,128)(2,1)S(1)}, u32[]{:S(2)}, u32[]{:S(2)}) collective-permute-start(bf16[256,1024]{1,0:T(8,128)(2,1)S(1)} %get-tuple-element.25), channel_id=1, source_target_pairs={{0,1},{1,0},{2,3},{3,2},{4,5},{5,4},{6,7},{7,6},{8,9},{9,8},{10,11... | collective-permute-start | bytes 1572872 | tf_op jit(solution)/shard_map/ppermute | solution.py:35
  19.2 2.5 %collective-permute-start.4 = (bf16[2,1024,128]{2,1,0:T(8,128)(2,1)S(1)}, bf16[2,1024,128]{2,1,0:T(8,128)(2,1)S(1)}, u32[]{:S(2)}, u32[]{:S(2)}) collective-permute-start(bf16[2,1024,128]{2,1,0:T(8,128)(2,1)S(1)} %collective-permute-done.newer), channel_id=1, source_target_pairs={{0,1},{1,0},{2,3},{3,2},{4,5},{5,4},{6,7},{7,6},{8,9},{9,8},{10,11... | collective-permute-start | bytes 1572872 | tf_op jit(solution)/shard_map/ppermute | solution.py:35
  19.3 2.5 %collective-permute-start.5 = (s32[1,128]{1,0:T(1,128)S(1)}, s32[1,128]{1,0:T(1,128)S(1)}, u32[]{:S(2)}, u32[]{:S(2)}) collective-permute-start(s32[1,128]{1,0:T(1,128)S(1)} %copy-done.2), channel_id=1, source_target_pairs={{0,1},{1,0},{2,3},{3,2},{4,5},{5,4},{6,7},{7,6},{8,9},{9,8},{10,11... | collective-permute-start | bytes 1544 | tf_op jit(solution)/shard_map/ppermute | solution.py:35
  23.1 6.7 %collective-permute-start.6 = (s32[200,128]{1,0:T(8,128)S(1)}, s32[200,128]{1,0:T(8,128)S(1)}, u32[]{:S(2)}, u32[]{:S(2)}) collective-permute-start(s32[200,128]{1,0:T(8,128)S(1)} %get-tuple-element.29), channel_id=1, source_target_pairs={{0,6},{2,4},{4,2},{6,0},{8,14},{10,12},{12,10},{14,8},{16,22},{18,... | collective-permute-start | bytes 307208 | tf_op jit(solution)/shard_map/ppermute | solution.py:35
  24.4 6.6 %collective-permute-start.7 = (s32[200,128]{1,0:T(8,128)S(1)}, s32[200,128]{1,0:T(8,128)S(1)}, u32[]{:S(2)}, u32[]{:S(2)}) collective-permute-start(s32[200,128]{1,0:T(8,128)S(1)} %get-tuple-element.30), channel_id=1, source_target_pairs={{0,4},{2,6},{4,0},{6,2},{8,12},{10,14},{12,8},{14,10},{16,20},{18,... | collective-permute-start | bytes 307208 | tf_op jit(solution)/shard_map/ppermute | solution.py:35
  24.4 6.6 %collective-permute-start.8 = (s32[200,128]{1,0:T(8,128)S(1)}, s32[200,128]{1,0:T(8,128)S(1)}, u32[]{:S(2)}, u32[]{:S(2)}) collective-permute-start(s32[200,128]{1,0:T(8,128)S(1)} %get-tuple-element.31), channel_id=1, source_target_pairs={{0,2},{2,0},{4,6},{6,4},{8,10},{10,8},{12,14},{14,12},{16,18},{18,... | collective-permute-start | bytes 307208 | tf_op jit(solution)/shard_map/ppermute | solution.py:35
  31.2 11.8 %collective-permute-start.10 = (s32[216,128]{1,0:T(8,128)S(1)}, s32[216,128]{1,0:T(8,128)S(1)}, u32[]{:S(2)}, u32[]{:S(2)}) collective-permute-start(s32[216,128]{1,0:T(8,128)S(1)} %get-tuple-element.37), channel_id=1, source_target_pairs={{0,16},{2,18},{4,20},{6,22},{8,24},{10,26},{12,28},{14,30},{16,0},... | collective-permute-start | bytes 331784 | tf_op jit(solution)/shard_map/ppermute | solution.py:35
  32.4 10.5 %collective-permute-start.11 = (s32[208,128]{1,0:T(8,128)S(1)}, s32[208,128]{1,0:T(8,128)S(1)}, u32[]{:S(2)}, u32[]{:S(2)}) collective-permute-start(s32[208,128]{1,0:T(8,128)S(1)} %get-tuple-element.38), channel_id=1, source_target_pairs={{0,24},{2,26},{4,28},{6,30},{8,16},{10,18},{12,20},{14,22},{16,8},... | collective-permute-start | bytes 319496 | tf_op jit(solution)/shard_map/ppermute | solution.py:35
  35.3 7.6 %collective-permute-start.9 = (s32[200,128]{1,0:T(8,128)S(1)}, s32[200,128]{1,0:T(8,128)S(1)}, u32[]{:S(2)}, u32[]{:S(2)}) collective-permute-start(s32[200,128]{1,0:T(8,128)S(1)} %get-tuple-element.36), channel_id=1, source_target_pairs={{0,8},{2,10},{4,12},{6,14},{8,0},{10,2},{12,4},{14,6},{16,24},{18,... | collective-permute-start | bytes 307208 | tf_op jit(solution)/shard_map/ppermute | solution.py:35
  43.8 5.7 %collective-permute-start.12 = (s32[200,128]{1,0:T(8,128)S(1)}, s32[200,128]{1,0:T(8,128)S(1)}, u32[]{:S(2)}, u32[]{:S(2)}) collective-permute-start(s32[200,128]{1,0:T(8,128)S(1)} %get-tuple-element.40), channel_id=1, source_target_pairs={{0,6},{2,4},{4,2},{6,0},{8,14},{10,12},{12,10},{14,8},{16,22},{18,... | collective-permute-start | bytes 307208 | tf_op jit(solution)/shard_map/ppermute | solution.py:35
  44.9 5.6 %collective-permute-start.13 = (s32[200,128]{1,0:T(8,128)S(1)}, s32[200,128]{1,0:T(8,128)S(1)}, u32[]{:S(2)}, u32[]{:S(2)}) collective-permute-start(s32[200,128]{1,0:T(8,128)S(1)} %get-tuple-element.41), channel_id=1, source_target_pairs={{0,4},{2,6},{4,0},{6,2},{8,12},{10,14},{12,8},{14,10},{16,20},{18,... | collective-permute-start | bytes 307208 | tf_op jit(solution)/shard_map/ppermute | solution.py:35
  45.3 5.3 %collective-permute-start.14 = (s32[200,128]{1,0:T(8,128)S(1)}, s32[200,128]{1,0:T(8,128)S(1)}, u32[]{:S(2)}, u32[]{:S(2)}) collective-permute-start(s32[200,128]{1,0:T(8,128)S(1)} %get-tuple-element.42), channel_id=1, source_target_pairs={{0,2},{2,0},{4,6},{6,4},{8,10},{10,8},{12,14},{14,12},{16,18},{18,... | collective-permute-start | bytes 307208 | tf_op jit(solution)/shard_map/ppermute | solution.py:35

commit v4 on v3

--- a/solution.py
+++ b/solution.py
@@ -10,7 +10,6 @@
 TICKS = 3
 PARTS = 2
 INNER = 4
-PADS = {2: 16, 3: 8}
 MASKS = tuple(range(INNER - 1, 0, -1))
 VMEM = pl.BlockSpec(memory_space=pltpu.VMEM)
 SMEM = pl.BlockSpec(memory_space=pltpu.SMEM)
@@ -35,22 +34,26 @@
     return lax.ppermute(value, axis, [(i, i ^ mask) for i in range(count)])
 
 
+def unit_of(eighths):
+    return jnp.exp2(eighths * 0.125 - 15.0)
+
+
 def pack(x, ref):
     ticks, half = x.shape[0], x.shape[1] // 2
     high = jnp.maximum(jnp.max(jnp.abs(x), axis=1, keepdims=True), 2.0**-100)
-    power = jnp.floor(jnp.log2(high)) + 1.0
-    q = jnp.clip(jnp.round(x * jnp.exp2(15.0 - power)), -32768.0, 32767.0).astype(jnp.int32)
+    eighths = jnp.floor(jnp.log2(high) * 8.0) + 1.0
+    q = jnp.clip(jnp.round(x * (1.0 / unit_of(eighths))), -32768.0, 32767.0).astype(jnp.int32)
     words = (q[:, :half] & 0xFFFF) | (q[:, half:] << 16)
     for t in range(ticks):
         ref[t * half : (t + 1) * half, :] = words[t]
-    scales = power.astype(jnp.int32)
+    scales = eighths.astype(jnp.int32)
     tail = jnp.concatenate([scales[t] for t in range(ticks)] + [jnp.zeros((8 - ticks, x.shape[2]), jnp.int32)], axis=0)
     ref[ticks * half : ticks * half + 8, :] = tail
 
 
 def unpack(ref, half):
     ticks = TICKS
-    unit = jnp.exp2(ref[ticks * half : ticks * half + 8, :].astype(jnp.float32) - 15.0)
+    unit = unit_of(ref[ticks * half : ticks * half + 8, :].astype(jnp.float32))
     values = []
     for t in range(ticks):
         words = ref[t * half : (t + 1) * half, :]
@@ -142,14 +145,9 @@
     total = mine[...]
     for ref in received:
         total = total + unpack(ref, half)
-    size = TICKS * half + 8
-    for i, out in enumerate(outs):
-        if i:
-            out[:size, :] = outs[0][:size, :]
-        else:
-            pack(total, out)
-        if out.shape[0] > size:
-            out[size:, :] = jnp.zeros((out.shape[0] - size, out.shape[1]), jnp.int32)
+    pack(total, outs[0])
+    for out in outs[1:]:
+        out[...] = outs[0][...]
 
 
 def inner_kernel(where, mine, *refs):
@@ -177,18 +175,26 @@
         pack(ref[...] + earlier, out)
 
 
-def finish_kernel(where, own, base, *refs):
-    received, (out, ready, sems) = refs[:-3], refs[-3:]
-    piece = base.shape[1]
+def write_rows(where, own, pieces, out, ready, sems):
     copies = []
-    for k, ref in zip((0, *MASKS), (base, *received)):
+    for i, (k, older) in enumerate(pieces):
+        piece = older.shape[1]
         first = pl.multiple_of((where[3] ^ k) * piece, piece)
-        older = unpack(ref, piece // 2) if k else ref[...]
-        ready[k] = own[:, pl.ds(first, piece), :] + older
-        copies.append(pltpu.make_async_copy(ready.at[k], out.at[:, pl.ds(first, piece), :], sems.at[k]))
+        ready[i] = own[:, pl.ds(first, piece), :] + older
+        copies.append(pltpu.make_async_copy(ready.at[i], out.at[:, pl.ds(first, piece), :], sems.at[i]))
         copies[-1].start()
     for copy in copies:
         copy.wait()
+
+
+def own_rows_kernel(where, own, base, out, ready, sems):
+    write_rows(where, own, [(0, base[...])], out, ready, sems)
+
+
+def finish_kernel(where, own, *refs):
+    received, out, ready, sems = refs[:-4], refs[-3], refs[-2], refs[-1]
+    half = own.shape[1] // INNER // 2
+    write_rows(where, own, ((k, unpack(ref, half)) for k, ref in zip(MASKS, received)), out, ready, sems)
 
 
 def among_members(values):
@@ -233,19 +239,30 @@
         [where, offsets, base, *others, *newer, *slots],
     )
     received = among_members(sends)
-    far = [jax.ShapeDtypeStruct((packed.shape[0] + PADS.get(k, 0), width), jnp.int32) for k in range(1, n_outer)]
-    sums = call(total_kernel, far, [mine, *received])
+    sums = call(total_kernel, [packed] * (n_outer - 1), [mine, *received])
     totals = [swapped(total, "lag", k * INNER) for k, total in enumerate(sums, 1)]
     inner = call(inner_kernel, [f32(piece)] * INNER, [where, mine, *received])
     older, *sends = call(prefix_kernel, [f32(piece)] + [packed] * (INNER - 1), [where, *inner, *totals])
     received = among_members(sends)
     [history_sum] = call(
+        own_rows_kernel,
+        [f32(rows)],
+        [where, own, older],
+        [pltpu.VMEM((1, TICKS, piece, width), jnp.float32), pltpu.SemaphoreType.DMA((1,))],
+        HBM,
+    )
+    history_sum = pl.pallas_call(
         finish_kernel,
-        [f32(rows)],
-        [where, own, older, *received],
-        [pltpu.VMEM((INNER, TICKS, piece, width), jnp.float32), pltpu.SemaphoreType.DMA((INNER,))],
-        HBM,
-    )
+        out_shape=f32(rows),
+        in_specs=[SMEM] + [VMEM] * INNER + [HBM],
+        out_specs=HBM,
+        scratch_shapes=[
+            pltpu.VMEM((INNER - 1, TICKS, piece, width), jnp.float32),
+            pltpu.SemaphoreType.DMA((INNER - 1,)),
+        ],
+        input_output_aliases={INNER + 1: 0},
+        compiler_params=LIMIT,
+    )(where, own, *received, history_sum)
     return jnp.transpose(history_sum, (1, 0, 2))[None]
 
 

time: 52.2 us -> 51.8 us (level)
  waiting for transfers between devices: 19.4 us -> 17.7 us
  Pallas kernels: 7.38 us -> 8.59 us
    ppermute x14, waiting for transfers between devices: 14 us -> 12.4 us  [swapped(): return lax.ppermute(value, axis, [(i, i ^ mask) for i in range(count)])]
    pallas_call x0 -> x1, Pallas kernels: none -> 1.4 us  [local(): pl.pallas_call(finish_kernel, out_shape=f32(rows), in_specs=[SMEM] + [VME...]
  transfers between devices with their start and end apart: 15 -> 15, of which waited for: 6 -> 7; matrix products, arithmetic and copies ran while one was open for 0% -> 0% of each run, Pallas kernels for 7% -> 9%
where the time goes in v4:
time: 51.8 us; the launch traced here: 51.6 us
  starting transfers between devices  19.9 us (38%)
  waiting for transfers between devices  17.7 us (34%)
  Pallas kernels  8.59 us (17%)
  local copies, waits for them, and re-layouts  4.63 us (9%)
  between operations  0.75 us (1%)
    ppermute x14, starting transfers between devices, swapped(): return lax.ppermute(value, axis, [(i, i ^ mask) for i in range(count)])  12.9 us
    ppermute x14, waiting for transfers between devices, swapped(): return lax.ppermute(value, axis, [(i, i ^ mask) for i in range(count)])  12.4 us
    pallas_call x7, Pallas kernels, call(): pl.pallas_call(kernel, out_shape=out_shape, in_specs=[SMEM if a.ndim == 1...  7.18 us
    ppermute x1, starting transfers between devices, local(): lax.ppermute(density_history[:TICKS - 1], 'lag', [(i, (i - 1) % n_lag) fo...  6.98 us
    ppermute x1, waiting for transfers between devices, local(): lax.ppermute(density_history[:TICKS - 1], 'lag', [(i, (i - 1) % n_lag) fo...  5.38 us
    unnamed x6, local copies, waits for them, and re-layouts  3.47 us
    pallas_call x1, Pallas kernels, local(): pl.pallas_call(finish_kernel, out_shape=f32(rows), in_specs=[SMEM] + [VME...  1.4 us
    slice x1, local copies, waits for them, and re-layouts, local(): density_history[:TICKS - 1]  1.08 us
  transfers between devices with their start and end apart: 15, of which 7 were waited for; matrix products, arithmetic and copies ran while one was open for 0% of the time, Pallas kernels for 9%

profile of v4, /device:TPU:0, one launch (start us, length us, event | category | flops | bytes accessed | tf_op | source)
XLA Modules:
  0.0 51.6 jit_solution(5494665748679692885)
XLA Ops:
  0.0 1.1 %slice.3 = bf16[2,1024,128]{2,1,0:T(8,128)(2,1)S(1)} slice(bf16[4,1024,128]{2,1,0:T(8,128)(2,1)} %own.1), slice={[0:2], [0:1024], [0:128]} | slice | bytes 1048576 | tf_op jit(solution)/shard_map/slice | solution.py:223
  1.1 7.0 %collective-permute-start = (bf16[2,1024,128]{2,1,0:T(8,128)(2,1)S(1)}, bf16[2,1024,128]{2,1,0:T(8,128)(2,1)S(1)}, u32[]{:S(2)}, u32[]{:S(2)}) collective-permute-start(bf16[2,1024,128]{2,1,0:T(8,128)(2,1)S(1)} %slice.3), channel_id=1, source_target_pairs={{0,30},{2,0},{4,2},{6,4},{8,6},{10,8},{12,10},{14,12},{16,14},{18,... | collective-permute-start | bytes 1572872 | tf_op jit(solution)/shard_map/ppermute | solution.py:223
  8.7 0.1 stack.23.where
  8.8 1.6 %copy-done = bf16[1,1024,1024]{2,1,0:T(8,128)(2,1)S(1)} copy-done((bf16[1,1024,1024]{2,1,0:T(8,128)(2,1)S(1)}, bf16[1,1024,1024]{2,1,0:T(8,128)(2,1)}, u32[]{:S(2)}) %copy-start) | copy-done | bytes 2097176
  10.4 1.2 %copy-done.1 = bf16[4,1024,128]{2,1,0:T(8,128)(2,1)S(1)} copy-done((bf16[4,1024,128]{2,1,0:T(8,128)(2,1)S(1)}, bf16[4,1024,128]{2,1,0:T(8,128)(2,1)}, u32[]{:S(2)}) %copy-start.1) | copy-done | bytes 1048600
  11.6 0.7 %copy-done.2 = s32[1,128]{1,0:T(1,128)S(1)} copy-done((s32[1,128]{1,0:T(1,128)S(1)}, s32[1,128]{1,0:T(1,128)}, u32[]{:S(2)}) %copy-start.2) | copy-done | bytes 536
  12.3 0.9 %shard_map.46 = (bf16[1024,384]{1,0:T(8,128)(2,1)S(1)}, bf16[256,1024]{1,0:T(8,128)(2,1)S(1)}, bf16[256,1024]{1,0:T(8,128)(2,1)S(1)}) custom-call(s32[5]{0:T(128)S(1)} %stack.23.where, s32[1]{0:T(128)S(6)} %copy.7.offset, bf16[1024,1024]{1,0:T(8,128)(2,1)S(1)} %bitcast.8, bf16[4,1024,128]{2,1,0:T(8,128)(2,1)S(1)} %copy-done.1, s32[1,128]{1,0:T(1,128)S(1)} %copy-done.2), custom_call_target="tpu_custom_call" | custom-call | tf_op jit(solution)/shard_map/pallas_call | solution.py:22
  13.3 0.5 collective-permute-start.1
  13.8 0.1 collective-permute-start.2
  13.9 5.4 %collective-permute-done.newer = bf16[2,1024,128]{2,1,0:T(8,128)(2,1)S(1)} collective-permute-done((bf16[2,1024,128]{2,1,0:T(8,128)(2,1)S(1)}, bf16[2,1024,128]{2,1,0:T(8,128)(2,1)S(1)}, u32[]{:S(2)}, u32[]{:S(2)}) %collective-permute-start) | collective-permute-done | bytes 524320 | tf_op jit(solution)/shard_map/ppermute | solution.py:223
  19.3 0.5 collective-permute-start.5
  19.8 1.9 %shard_map.47.base = f32[3,512,128]{2,1,0:T(8,128)S(1)} custom-call(s32[5]{0:T(128)S(1)} %stack.23.where, s32[1]{0:T(128)S(6)} %copy.7.offset, bf16[1024,1024]{1,0:T(8,128)(2,1)S(1)} %bitcast.9, bf16[2,1024,128]{2,1,0:T(8,128)(2,1)S(1)} %collective-permute-done.newer, s32[1,128]{1,0:T(1,128)S(1)} %copy-done.2, ...), custom_call_target="tpu_custom_call" | custom-call | tf_op jit(solution)/shard_map/pallas_call | solution.py:22
  21.7 1.3 %shard_map.48 = (f32[3,512,128]{2,1,0:T(8,128)S(1)}, f32[3,128,128]{2,1,0:T(8,128)S(1)}, s32[200,128]{1,0:T(8,128)S(1)}, s32[200,128]{1,0:T(8,128)S(1)}, s32[200,128]{1,0:T(8,128)S(1)}) custom-call(s32[5]{0:T(128)S(1)} %stack.23.where, s32[1]{0:T(128)S(6)} %copy.7.offset, f32[3,512,128]{2,1,0:T(8,128)S(1)} %shard_map.47.base, ...), custom_call_target="tpu_custom_call" | custom-call | tf_op jit(solution)/shard_map/pallas_call | solution.py:22
  23.1 1.3 %collective-permute-start.6 = (s32[200,128]{1,0:T(8,128)S(1)}, s32[200,128]{1,0:T(8,128)S(1)}, u32[]{:S(2)}, u32[]{:S(2)}) collective-permute-start(s32[200,128]{1,0:T(8,128)S(1)} %get-tuple-element.29), channel_id=1, source_target_pairs={{0,6},{2,4},{4,2},{6,0},{8,14},{10,12},{12,10},{14,8},{16,22},{18,... | collective-permute-start | bytes 307208 | tf_op jit(solution)/shard_map/ppermute | solution.py:34
  24.4 2.2 %collective-permute-start.8 = (s32[200,128]{1,0:T(8,128)S(1)}, s32[200,128]{1,0:T(8,128)S(1)}, u32[]{:S(2)}, u32[]{:S(2)}) collective-permute-start(s32[200,128]{1,0:T(8,128)S(1)} %get-tuple-element.31), channel_id=1, source_target_pairs={{0,2},{2,0},{4,6},{6,4},{8,10},{10,8},{12,14},{14,12},{16,18},{18,... | collective-permute-start | bytes 307208 | tf_op jit(solution)/shard_map/ppermute | solution.py:34
  26.6 3.2 %collective-permute-done.6.refs_0_ = s32[200,128]{1,0:T(8,128)S(1)} collective-permute-done((s32[200,128]{1,0:T(8,128)S(1)}, s32[200,128]{1,0:T(8,128)S(1)}, u32[]{:S(2)}, u32[]{:S(2)}) %collective-permute-start.6) | collective-permute-done | bytes 102432 | tf_op jit(solution)/shard_map/ppermute | solution.py:34
  29.8 1.2 %collective-permute-done.7.refs_1_ = s32[200,128]{1,0:T(8,128)S(1)} collective-permute-done((s32[200,128]{1,0:T(8,128)S(1)}, s32[200,128]{1,0:T(8,128)S(1)}, u32[]{:S(2)}, u32[]{:S(2)}) %collective-permute-start.7) | collective-permute-done | bytes 102432 | tf_op jit(solution)/shard_map/ppermute | solution.py:34
  31.0 0.2 shard_map.50
  31.2 1.3 %collective-permute-start.10 = (s32[200,128]{1,0:T(8,128)S(1)}, s32[200,128]{1,0:T(8,128)S(1)}, u32[]{:S(2)}, u32[]{:S(2)}) collective-permute-start(s32[200,128]{1,0:T(8,128)S(1)} %get-tuple-element.37), channel_id=1, source_target_pairs={{0,16},{2,18},{4,20},{6,22},{8,24},{10,26},{12,28},{14,30},{16,0},... | collective-permute-start | bytes 307208 | tf_op jit(solution)/shard_map/ppermute | solution.py:34
  32.5 2.9 %collective-permute-start.11 = (s32[200,128]{1,0:T(8,128)S(1)}, s32[200,128]{1,0:T(8,128)S(1)}, u32[]{:S(2)}, u32[]{:S(2)}) collective-permute-start(s32[200,128]{1,0:T(8,128)S(1)} %get-tuple-element.38), channel_id=1, source_target_pairs={{0,24},{2,26},{4,28},{6,30},{8,16},{10,18},{12,20},{14,22},{16,8},... | collective-permute-start | bytes 307208 | tf_op jit(solution)/shard_map/ppermute | solution.py:34
  35.3 0.5 collective-permute-start.9
  35.8 0.8 %shard_map.49 = (f32[3,128,128]{2,1,0:T(8,128)S(1)}, f32[3,128,128]{2,1,0:T(8,128)S(1)}, f32[3,128,128]{2,1,0:T(8,128)S(1)}, f32[3,128,128]{2,1,0:T(8,128)S(1)}) custom-call(s32[5]{0:T(128)S(1)} %stack.23.where, f32[3,128,128]{2,1,0:T(8,128)S(1)} %get-tuple-element.28.mine, s32[200,128]{1,0:T(8,128)S(1)} %collective-permute-done.6.refs_0_, ...), custom_call_target="tpu_custom_call" | custom-call | tf_op jit(solution)/shard_map/pallas_call | solution.py:22
  36.6 5.7 %collective-permute-done.10.refs_5_ = s32[200,128]{1,0:T(8,128)S(1)} collective-permute-done((s32[200,128]{1,0:T(8,128)S(1)}, s32[200,128]{1,0:T(8,128)S(1)}, u32[]{:S(2)}, u32[]{:S(2)}) %collective-permute-start.10) | collective-permute-done | bytes 102432 | tf_op jit(solution)/shard_map/ppermute | solution.py:34
  42.3 0.3 collective-permute-done.9.refs_4_
  42.6 0.8 %shard_map.51 = (f32[3,128,128]{2,1,0:T(8,128)S(1)}, s32[200,128]{1,0:T(8,128)S(1)}, s32[200,128]{1,0:T(8,128)S(1)}, s32[200,128]{1,0:T(8,128)S(1)}) custom-call(s32[5]{0:T(128)S(1)} %stack.23.where, f32[3,128,128]{2,1,0:T(8,128)S(1)} %get-tuple-element.32.refs_0_, f32[3,128,128]{2,1,0:T(8,128)S(1)} %get-tuple-element.33.refs_1_, ...), custom_call_target="tpu_custom_call" | custom-call | tf_op jit(solution)/shard_map/pallas_call | solution.py:22
  43.5 1.1 %collective-permute-start.12 = (s32[200,128]{1,0:T(8,128)S(1)}, s32[200,128]{1,0:T(8,128)S(1)}, u32[]{:S(2)}, u32[]{:S(2)}) collective-permute-start(s32[200,128]{1,0:T(8,128)S(1)} %get-tuple-element.39), channel_id=1, source_target_pairs={{0,6},{2,4},{4,2},{6,0},{8,14},{10,12},{12,10},{14,8},{16,22},{18,... | collective-permute-start | bytes 307208 | tf_op jit(solution)/shard_map/ppermute | solution.py:34
  44.6 0.7 %collective-permute-start.13 = (s32[200,128]{1,0:T(8,128)S(1)}, s32[200,128]{1,0:T(8,128)S(1)}, u32[]{:S(2)}, u32[]{:S(2)}) collective-permute-start(s32[200,128]{1,0:T(8,128)S(1)} %get-tuple-element.40), channel_id=1, source_target_pairs={{0,4},{2,6},{4,0},{6,2},{8,12},{10,14},{12,8},{14,10},{16,20},{18,... | collective-permute-start | bytes 307208 | tf_op jit(solution)/shard_map/ppermute | solution.py:34
  45.2 1.8 %collective-permute-start.14 = (s32[200,128]{1,0:T(8,128)S(1)}, s32[200,128]{1,0:T(8,128)S(1)}, u32[]{:S(2)}, u32[]{:S(2)}) collective-permute-start(s32[200,128]{1,0:T(8,128)S(1)} %get-tuple-element.41), channel_id=1, source_target_pairs={{0,2},{2,0},{4,6},{6,4},{8,10},{10,8},{12,14},{14,12},{16,18},{18,... | collective-permute-start | bytes 307208 | tf_op jit(solution)/shard_map/ppermute | solution.py:34
  47.0 1.2 %shard_map.52.refs_3_ = f32[3,512,128]{2,1,0:T(8,128)} custom-call(s32[5]{0:T(128)S(1)} %stack.23.where, f32[3,512,128]{2,1,0:T(8,128)S(1)} %get-tuple-element.27.own, f32[3,128,128]{2,1,0:T(8,128)S(1)} %get-tuple-element.42.base), custom_call_target="tpu_custom_call" | custom-call | tf_op jit(solution)/shard_map/pallas_call | solution.py:22
  48.3 0.9 %collective-permute-done.12.refs_0_ = s32[200,128]{1,0:T(8,128)S(1)} collective-permute-done((s32[200,128]{1,0:T(8,128)S(1)}, s32[200,128]{1,0:T(8,128)S(1)}, u32[]{:S(2)}, u32[]{:S(2)}) %collective-permute-start.12) | collective-permute-done | bytes 102432 | tf_op jit(solution)/shard_map/ppermute | solution.py:34
  49.2 1.0 %collective-permute-done.13.refs_1_ = s32[200,128]{1,0:T(8,128)S(1)} collective-permute-done((s32[200,128]{1,0:T(8,128)S(1)}, s32[200,128]{1,0:T(8,128)S(1)}, u32[]{:S(2)}, u32[]{:S(2)}) %collective-permute-start.13) | collective-permute-done | bytes 102432 | tf_op jit(solution)/shard_map/ppermute | solution.py:34
  50.2 1.4 %shard_map.53 = f32[3,512,128]{2,1,0:T(8,128)} custom-call(s32[5]{0:T(128)S(1)} %stack.23.where, f32[3,512,128]{2,1,0:T(8,128)S(1)} %get-tuple-element.27.own, s32[200,128]{1,0:T(8,128)S(1)} %collective-permute-done.12.refs_0_, s32[200,128]{1,0:T(8,128)S(1)} %collective-permute-done.13.refs_1_, ...), custom_call_target="tpu_custom_call", output_to_operand_aliasing={{}: (5, {})} | custom-call | tf_op jit(solution)/shard_map/pallas_call | solution.py:254
  (14 shorter events, 0.1 us)
Async XLA Ops:
  1.1 18.2 %collective-permute-start = (bf16[2,1024,128]{2,1,0:T(8,128)(2,1)S(1)}, bf16[2,1024,128]{2,1,0:T(8,128)(2,1)S(1)}, u32[]{:S(2)}, u32[]{:S(2)}) collective-permute-start(bf16[2,1024,128]{2,1,0:T(8,128)(2,1)S(1)} %slice.3), channel_id=1, source_target_pairs={{0,30},{2,0},{4,2},{6,4},{8,6},{10,8},{12,10},{14,12},{16,14},{18,... | collective-permute-start | bytes 1572872 | tf_op jit(solution)/shard_map/ppermute | solution.py:223
  8.8 1.6 %copy-start = (bf16[1,1024,1024]{2,1,0:T(8,128)(2,1)S(1)}, bf16[1,1024,1024]{2,1,0:T(8,128)(2,1)}, u32[]{:S(2)}) copy-start(bf16[1,1024,1024]{2,1,0:T(8,128)(2,1)} %param.4) | copy-start | bytes 6291460
  10.4 1.2 %copy-start.1 = (bf16[4,1024,128]{2,1,0:T(8,128)(2,1)S(1)}, bf16[4,1024,128]{2,1,0:T(8,128)(2,1)}, u32[]{:S(2)}) copy-start(bf16[4,1024,128]{2,1,0:T(8,128)(2,1)} %own.1) | copy-start | bytes 3145732
  11.6 0.7 %copy-start.2 = (s32[1,128]{1,0:T(1,128)S(1)}, s32[1,128]{1,0:T(1,128)}, u32[]{:S(2)}) copy-start(s32[1,128]{1,0:T(1,128)} %slots.3) | copy-start | bytes 1540
  13.2 6.6 %collective-permute-start.3 = (bf16[1024,384]{1,0:T(8,128)(2,1)S(1)}, bf16[1024,384]{1,0:T(8,128)(2,1)S(1)}, u32[]{:S(2)}, u32[]{:S(2)}) collective-permute-start(bf16[1024,384]{1,0:T(8,128)(2,1)S(1)} %get-tuple-element.26.refs_2_), channel_id=1, source_target_pairs={{0,1},{1,0},{2,3},{3,2},{4,5},{5,4},{6,7},{7,6},{8,9},{9,8},{10,11... | collective-permute-start | bytes 2359304 | tf_op jit(solution)/shard_map/ppermute | solution.py:34
  13.3 6.5 %collective-permute-start.1 = (bf16[256,1024]{1,0:T(8,128)(2,1)S(1)}, bf16[256,1024]{1,0:T(8,128)(2,1)S(1)}, u32[]{:S(2)}, u32[]{:S(2)}) collective-permute-start(bf16[256,1024]{1,0:T(8,128)(2,1)S(1)} %get-tuple-element.24), channel_id=1, source_target_pairs={{0,1},{1,0},{2,3},{3,2},{4,5},{5,4},{6,7},{7,6},{8,9},{9,8},{10,11... | collective-permute-start | bytes 1572872 | tf_op jit(solution)/shard_map/ppermute | solution.py:34
  13.8 6.0 %collective-permute-start.2 = (bf16[256,1024]{1,0:T(8,128)(2,1)S(1)}, bf16[256,1024]{1,0:T(8,128)(2,1)S(1)}, u32[]{:S(2)}, u32[]{:S(2)}) collective-permute-start(bf16[256,1024]{1,0:T(8,128)(2,1)S(1)} %get-tuple-element.25), channel_id=1, source_target_pairs={{0,1},{1,0},{2,3},{3,2},{4,5},{5,4},{6,7},{7,6},{8,9},{9,8},{10,11... | collective-permute-start | bytes 1572872 | tf_op jit(solution)/shard_map/ppermute | solution.py:34
  19.2 2.5 %collective-permute-start.4 = (bf16[2,1024,128]{2,1,0:T(8,128)(2,1)S(1)}, bf16[2,1024,128]{2,1,0:T(8,128)(2,1)S(1)}, u32[]{:S(2)}, u32[]{:S(2)}) collective-permute-start(bf16[2,1024,128]{2,1,0:T(8,128)(2,1)S(1)} %collective-permute-done.newer), channel_id=1, source_target_pairs={{0,1},{1,0},{2,3},{3,2},{4,5},{5,4},{6,7},{7,6},{8,9},{9,8},{10,11... | collective-permute-start | bytes 1572872 | tf_op jit(solution)/shard_map/ppermute | solution.py:34
  19.3 2.5 %collective-permute-start.5 = (s32[1,128]{1,0:T(1,128)S(1)}, s32[1,128]{1,0:T(1,128)S(1)}, u32[]{:S(2)}, u32[]{:S(2)}) collective-permute-start(s32[1,128]{1,0:T(1,128)S(1)} %copy-done.2), channel_id=1, source_target_pairs={{0,1},{1,0},{2,3},{3,2},{4,5},{5,4},{6,7},{7,6},{8,9},{9,8},{10,11... | collective-permute-start | bytes 1544 | tf_op jit(solution)/shard_map/ppermute | solution.py:34
  23.1 6.7 %collective-permute-start.6 = (s32[200,128]{1,0:T(8,128)S(1)}, s32[200,128]{1,0:T(8,128)S(1)}, u32[]{:S(2)}, u32[]{:S(2)}) collective-permute-start(s32[200,128]{1,0:T(8,128)S(1)} %get-tuple-element.29), channel_id=1, source_target_pairs={{0,6},{2,4},{4,2},{6,0},{8,14},{10,12},{12,10},{14,8},{16,22},{18,... | collective-permute-start | bytes 307208 | tf_op jit(solution)/shard_map/ppermute | solution.py:34
  24.4 6.6 %collective-permute-start.7 = (s32[200,128]{1,0:T(8,128)S(1)}, s32[200,128]{1,0:T(8,128)S(1)}, u32[]{:S(2)}, u32[]{:S(2)}) collective-permute-start(s32[200,128]{1,0:T(8,128)S(1)} %get-tuple-element.30), channel_id=1, source_target_pairs={{0,4},{2,6},{4,0},{6,2},{8,12},{10,14},{12,8},{14,10},{16,20},{18,... | collective-permute-start | bytes 307208 | tf_op jit(solution)/shard_map/ppermute | solution.py:34
  24.4 6.6 %collective-permute-start.8 = (s32[200,128]{1,0:T(8,128)S(1)}, s32[200,128]{1,0:T(8,128)S(1)}, u32[]{:S(2)}, u32[]{:S(2)}) collective-permute-start(s32[200,128]{1,0:T(8,128)S(1)} %get-tuple-element.31), channel_id=1, source_target_pairs={{0,2},{2,0},{4,6},{6,4},{8,10},{10,8},{12,14},{14,12},{16,18},{18,... | collective-permute-start | bytes 307208 | tf_op jit(solution)/shard_map/ppermute | solution.py:34
  31.2 11.1 %collective-permute-start.10 = (s32[200,128]{1,0:T(8,128)S(1)}, s32[200,128]{1,0:T(8,128)S(1)}, u32[]{:S(2)}, u32[]{:S(2)}) collective-permute-start(s32[200,128]{1,0:T(8,128)S(1)} %get-tuple-element.37), channel_id=1, source_target_pairs={{0,16},{2,18},{4,20},{6,22},{8,24},{10,26},{12,28},{14,30},{16,0},... | collective-permute-start | bytes 307208 | tf_op jit(solution)/shard_map/ppermute | solution.py:34
  32.5 9.8 %collective-permute-start.11 = (s32[200,128]{1,0:T(8,128)S(1)}, s32[200,128]{1,0:T(8,128)S(1)}, u32[]{:S(2)}, u32[]{:S(2)}) collective-permute-start(s32[200,128]{1,0:T(8,128)S(1)} %get-tuple-element.38), channel_id=1, source_target_pairs={{0,24},{2,26},{4,28},{6,30},{8,16},{10,18},{12,20},{14,22},{16,8},... | collective-permute-start | bytes 307208 | tf_op jit(solution)/shard_map/ppermute | solution.py:34
  35.3 7.3 %collective-permute-start.9 = (s32[200,128]{1,0:T(8,128)S(1)}, s32[200,128]{1,0:T(8,128)S(1)}, u32[]{:S(2)}, u32[]{:S(2)}) collective-permute-start(s32[200,128]{1,0:T(8,128)S(1)} %get-tuple-element.36), channel_id=1, source_target_pairs={{0,8},{2,10},{4,12},{6,14},{8,0},{10,2},{12,4},{14,6},{16,24},{18,... | collective-permute-start | bytes 307208 | tf_op jit(solution)/shard_map/ppermute | solution.py:34
  43.5 5.7 %collective-permute-start.12 = (s32[200,128]{1,0:T(8,128)S(1)}, s32[200,128]{1,0:T(8,128)S(1)}, u32[]{:S(2)}, u32[]{:S(2)}) collective-permute-start(s32[200,128]{1,0:T(8,128)S(1)} %get-tuple-element.39), channel_id=1, source_target_pairs={{0,6},{2,4},{4,2},{6,0},{8,14},{10,12},{12,10},{14,8},{16,22},{18,... | collective-permute-start | bytes 307208 | tf_op jit(solution)/shard_map/ppermute | solution.py:34
  44.6 5.6 %collective-permute-start.13 = (s32[200,128]{1,0:T(8,128)S(1)}, s32[200,128]{1,0:T(8,128)S(1)}, u32[]{:S(2)}, u32[]{:S(2)}) collective-permute-start(s32[200,128]{1,0:T(8,128)S(1)} %get-tuple-element.40), channel_id=1, source_target_pairs={{0,4},{2,6},{4,0},{6,2},{8,12},{10,14},{12,8},{14,10},{16,20},{18,... | collective-permute-start | bytes 307208 | tf_op jit(solution)/shard_map/ppermute | solution.py:34
  45.2 4.9 %collective-permute-start.14 = (s32[200,128]{1,0:T(8,128)S(1)}, s32[200,128]{1,0:T(8,128)S(1)}, u32[]{:S(2)}, u32[]{:S(2)}) collective-permute-start(s32[200,128]{1,0:T(8,128)S(1)} %get-tuple-element.41), channel_id=1, source_target_pairs={{0,2},{2,0},{4,6},{6,4},{8,10},{10,8},{12,14},{14,12},{16,18},{18,... | collective-permute-start | bytes 307208 | tf_op jit(solution)/shard_map/ppermute | solution.py:34

commit v5 on v4

--- a/solution.py
+++ b/solution.py
@@ -168,8 +168,8 @@
     half = base.shape[1] // 2
     group = where[4]
     earlier = jnp.zeros(base.shape, jnp.float32)
-    for k, ref in enumerate(totals, 1):
-        earlier = earlier + jnp.where((group ^ k) < group, unpack(ref, half), 0.0)
+    for k, ref in zip(range(len(totals), 0, -1), totals):
+        earlier = earlier + jnp.where(group >= k, unpack(ref, half), 0.0)
     base[...] = inner[0][...] + earlier
     for ref, out in zip(inner[1:], sends):
         pack(ref[...] + earlier, out)
@@ -240,7 +240,9 @@
     )
     received = among_members(sends)
     sums = call(total_kernel, [packed] * (n_outer - 1), [mine, *received])
-    totals = [swapped(total, "lag", k * INNER) for k, total in enumerate(sums, 1)]
+    totals = [
+        lax.ppermute(total, "lag", [(i, (i + k * INNER) % n_lag) for i in range(n_lag)]) for k, total in zip(range(n_outer - 1, 0, -1), sums)
+    ]
     inner = call(inner_kernel, [f32(piece)] * INNER, [where, mine, *received])
     older, *sends = call(prefix_kernel, [f32(piece)] + [packed] * (INNER - 1), [where, *inner, *totals])
     received = among_members(sends)

time: 51.8 us -> 51.9 us (level)
    ppermute x14 -> x11, waiting for transfers between devices: 12.4 us -> 6.33 us  [swapped(): return lax.ppermute(value, axis, [(i, i ^ mask) for i in range(count)])]
    ppermute x0 -> x3, waiting for transfers between devices: none -> 5.69 us  [local(): lax.ppermute(total, 'lag', [(i, (i + k * INNER) % n_lag) for i in range(n...]
    ppermute x0 -> x3, starting transfers between devices: none -> 5.08 us  [local(): lax.ppermute(total, 'lag', [(i, (i + k * INNER) % n_lag) for i in range(n...]
    ppermute x14 -> x11, starting transfers between devices: 12.9 us -> 8.26 us  [swapped(): return lax.ppermute(value, axis, [(i, i ^ mask) for i in range(count)])]
where the time goes in v5:
time: 51.9 us; the launch traced here: 51.7 us
  starting transfers between devices  20.3 us (39%)
  waiting for transfers between devices  17.4 us (34%)
  Pallas kernels  8.59 us (17%)
  local copies, waits for them, and re-layouts  4.63 us (9%)
  between operations  0.75 us (1%)
    ppermute x11, starting transfers between devices, swapped(): return lax.ppermute(value, axis, [(i, i ^ mask) for i in range(count)])  8.26 us
    pallas_call x7, Pallas kernels, call(): pl.pallas_call(kernel, out_shape=out_shape, in_specs=[SMEM if a.ndim == 1...  7.18 us
    ppermute x1, starting transfers between devices, local(): lax.ppermute(density_history[:TICKS - 1], 'lag', [(i, (i - 1) % n_lag) fo...  6.98 us
    ppermute x11, waiting for transfers between devices, swapped(): return lax.ppermute(value, axis, [(i, i ^ mask) for i in range(count)])  6.33 us
    ppermute x3, waiting for transfers between devices, local(): lax.ppermute(total, 'lag', [(i, (i + k * INNER) % n_lag) for i in range(n...  5.69 us
    ppermute x1, waiting for transfers between devices, local(): lax.ppermute(density_history[:TICKS - 1], 'lag', [(i, (i - 1) % n_lag) fo...  5.38 us
    ppermute x3, starting transfers between devices, local(): lax.ppermute(total, 'lag', [(i, (i + k * INNER) % n_lag) for i in range(n...  5.08 us
    unnamed x6, local copies, waits for them, and re-layouts  3.47 us
  transfers between devices with their start and end apart: 15, of which 7 were waited for; matrix products, arithmetic and copies ran while one was open for 0% of the time, Pallas kernels for 9%

profile of v5, /device:TPU:0, one launch (start us, length us, event | category | flops | bytes accessed | tf_op | source)
XLA Modules:
  0.0 51.7 jit_solution(529646494132976087)
XLA Ops:
  0.0 1.1 %slice.3 = bf16[2,1024,128]{2,1,0:T(8,128)(2,1)S(1)} slice(bf16[4,1024,128]{2,1,0:T(8,128)(2,1)} %own.1), slice={[0:2], [0:1024], [0:128]} | slice | bytes 1048576 | tf_op jit(solution)/shard_map/slice | solution.py:223
  1.1 7.0 %collective-permute-start = (bf16[2,1024,128]{2,1,0:T(8,128)(2,1)S(1)}, bf16[2,1024,128]{2,1,0:T(8,128)(2,1)S(1)}, u32[]{:S(2)}, u32[]{:S(2)}) collective-permute-start(bf16[2,1024,128]{2,1,0:T(8,128)(2,1)S(1)} %slice.3), channel_id=1, source_target_pairs={{0,30},{2,0},{4,2},{6,4},{8,6},{10,8},{12,10},{14,12},{16,14},{18,... | collective-permute-start | bytes 1572872 | tf_op jit(solution)/shard_map/ppermute | solution.py:223
  8.7 0.1 stack.23.where
  8.8 1.6 %copy-done = bf16[1,1024,1024]{2,1,0:T(8,128)(2,1)S(1)} copy-done((bf16[1,1024,1024]{2,1,0:T(8,128)(2,1)S(1)}, bf16[1,1024,1024]{2,1,0:T(8,128)(2,1)}, u32[]{:S(2)}) %copy-start) | copy-done | bytes 2097176
  10.4 1.2 %copy-done.1 = bf16[4,1024,128]{2,1,0:T(8,128)(2,1)S(1)} copy-done((bf16[4,1024,128]{2,1,0:T(8,128)(2,1)S(1)}, bf16[4,1024,128]{2,1,0:T(8,128)(2,1)}, u32[]{:S(2)}) %copy-start.1) | copy-done | bytes 1048600
  11.6 0.7 %copy-done.2 = s32[1,128]{1,0:T(1,128)S(1)} copy-done((s32[1,128]{1,0:T(1,128)S(1)}, s32[1,128]{1,0:T(1,128)}, u32[]{:S(2)}) %copy-start.2) | copy-done | bytes 536
  12.3 0.9 %shard_map.46 = (bf16[1024,384]{1,0:T(8,128)(2,1)S(1)}, bf16[256,1024]{1,0:T(8,128)(2,1)S(1)}, bf16[256,1024]{1,0:T(8,128)(2,1)S(1)}) custom-call(s32[5]{0:T(128)S(1)} %stack.23.where, s32[1]{0:T(128)S(6)} %copy.7.offset, bf16[1024,1024]{1,0:T(8,128)(2,1)S(1)} %bitcast.8, bf16[4,1024,128]{2,1,0:T(8,128)(2,1)S(1)} %copy-done.1, s32[1,128]{1,0:T(1,128)S(1)} %copy-done.2), custom_call_target="tpu_custom_call" | custom-call | tf_op jit(solution)/shard_map/pallas_call | solution.py:22
  13.3 0.5 collective-permute-start.1
  13.8 0.1 collective-permute-start.2
  13.9 5.4 %collective-permute-done.newer = bf16[2,1024,128]{2,1,0:T(8,128)(2,1)S(1)} collective-permute-done((bf16[2,1024,128]{2,1,0:T(8,128)(2,1)S(1)}, bf16[2,1024,128]{2,1,0:T(8,128)(2,1)S(1)}, u32[]{:S(2)}, u32[]{:S(2)}) %collective-permute-start) | collective-permute-done | bytes 524320 | tf_op jit(solution)/shard_map/ppermute | solution.py:223
  19.3 0.5 collective-permute-start.5
  19.8 1.9 %shard_map.47.base = f32[3,512,128]{2,1,0:T(8,128)S(1)} custom-call(s32[5]{0:T(128)S(1)} %stack.23.where, s32[1]{0:T(128)S(6)} %copy.7.offset, bf16[1024,1024]{1,0:T(8,128)(2,1)S(1)} %bitcast.9, bf16[2,1024,128]{2,1,0:T(8,128)(2,1)S(1)} %collective-permute-done.newer, s32[1,128]{1,0:T(1,128)S(1)} %copy-done.2, ...), custom_call_target="tpu_custom_call" | custom-call | tf_op jit(solution)/shard_map/pallas_call | solution.py:22
  21.7 1.3 %shard_map.48 = (f32[3,512,128]{2,1,0:T(8,128)S(1)}, f32[3,128,128]{2,1,0:T(8,128)S(1)}, s32[200,128]{1,0:T(8,128)S(1)}, s32[200,128]{1,0:T(8,128)S(1)}, s32[200,128]{1,0:T(8,128)S(1)}) custom-call(s32[5]{0:T(128)S(1)} %stack.23.where, s32[1]{0:T(128)S(6)} %copy.7.offset, f32[3,512,128]{2,1,0:T(8,128)S(1)} %shard_map.47.base, ...), custom_call_target="tpu_custom_call" | custom-call | tf_op jit(solution)/shard_map/pallas_call | solution.py:22
  23.1 1.3 %collective-permute-start.6 = (s32[200,128]{1,0:T(8,128)S(1)}, s32[200,128]{1,0:T(8,128)S(1)}, u32[]{:S(2)}, u32[]{:S(2)}) collective-permute-start(s32[200,128]{1,0:T(8,128)S(1)} %get-tuple-element.29), channel_id=1, source_target_pairs={{0,6},{2,4},{4,2},{6,0},{8,14},{10,12},{12,10},{14,8},{16,22},{18,... | collective-permute-start | bytes 307208 | tf_op jit(solution)/shard_map/ppermute | solution.py:34
  24.4 2.2 %collective-permute-start.8 = (s32[200,128]{1,0:T(8,128)S(1)}, s32[200,128]{1,0:T(8,128)S(1)}, u32[]{:S(2)}, u32[]{:S(2)}) collective-permute-start(s32[200,128]{1,0:T(8,128)S(1)} %get-tuple-element.31), channel_id=1, source_target_pairs={{0,2},{2,0},{4,6},{6,4},{8,10},{10,8},{12,14},{14,12},{16,18},{18,... | collective-permute-start | bytes 307208 | tf_op jit(solution)/shard_map/ppermute | solution.py:34
  26.6 3.2 %collective-permute-done.6.refs_0_ = s32[200,128]{1,0:T(8,128)S(1)} collective-permute-done((s32[200,128]{1,0:T(8,128)S(1)}, s32[200,128]{1,0:T(8,128)S(1)}, u32[]{:S(2)}, u32[]{:S(2)}) %collective-permute-start.6) | collective-permute-done | bytes 102432 | tf_op jit(solution)/shard_map/ppermute | solution.py:34
  29.8 1.2 %collective-permute-done.7.refs_1_ = s32[200,128]{1,0:T(8,128)S(1)} collective-permute-done((s32[200,128]{1,0:T(8,128)S(1)}, s32[200,128]{1,0:T(8,128)S(1)}, u32[]{:S(2)}, u32[]{:S(2)}) %collective-permute-start.7) | collective-permute-done | bytes 102432 | tf_op jit(solution)/shard_map/ppermute | solution.py:34
  31.0 0.2 shard_map.50
  31.2 1.3 %collective-permute-start.10 = (s32[200,128]{1,0:T(8,128)S(1)}, s32[200,128]{1,0:T(8,128)S(1)}, u32[]{:S(2)}, u32[]{:S(2)}) collective-permute-start(s32[200,128]{1,0:T(8,128)S(1)} %get-tuple-element.37), channel_id=1, source_target_pairs={{0,16},{2,18},{4,20},{6,22},{8,24},{10,26},{12,28},{14,30},{16,0},... | collective-permute-start | bytes 307208 | tf_op jit(solution)/shard_map/ppermute | solution.py:244
  32.5 3.4 %collective-permute-start.11 = (s32[200,128]{1,0:T(8,128)S(1)}, s32[200,128]{1,0:T(8,128)S(1)}, u32[]{:S(2)}, u32[]{:S(2)}) collective-permute-start(s32[200,128]{1,0:T(8,128)S(1)} %get-tuple-element.38), channel_id=1, source_target_pairs={{0,8},{2,10},{4,12},{6,14},{8,16},{10,18},{12,20},{14,22},{16,24},... | collective-permute-start | bytes 307208 | tf_op jit(solution)/shard_map/ppermute | solution.py:244
  35.8 0.4 collective-permute-start.9
  36.3 0.8 %shard_map.49 = (f32[3,128,128]{2,1,0:T(8,128)S(1)}, f32[3,128,128]{2,1,0:T(8,128)S(1)}, f32[3,128,128]{2,1,0:T(8,128)S(1)}, f32[3,128,128]{2,1,0:T(8,128)S(1)}) custom-call(s32[5]{0:T(128)S(1)} %stack.23.where, f32[3,128,128]{2,1,0:T(8,128)S(1)} %get-tuple-element.28.mine, s32[200,128]{1,0:T(8,128)S(1)} %collective-permute-done.6.refs_0_, ...), custom_call_target="tpu_custom_call" | custom-call | tf_op jit(solution)/shard_map/pallas_call | solution.py:22
  37.0 5.2 %collective-permute-done.10.refs_5_ = s32[200,128]{1,0:T(8,128)S(1)} collective-permute-done((s32[200,128]{1,0:T(8,128)S(1)}, s32[200,128]{1,0:T(8,128)S(1)}, u32[]{:S(2)}, u32[]{:S(2)}) %collective-permute-start.10) | collective-permute-done | bytes 102432 | tf_op jit(solution)/shard_map/ppermute | solution.py:244
  42.3 0.4 collective-permute-done.9.refs_4_
  42.7 0.8 %shard_map.51 = (f32[3,128,128]{2,1,0:T(8,128)S(1)}, s32[200,128]{1,0:T(8,128)S(1)}, s32[200,128]{1,0:T(8,128)S(1)}, s32[200,128]{1,0:T(8,128)S(1)}) custom-call(s32[5]{0:T(128)S(1)} %stack.23.where, f32[3,128,128]{2,1,0:T(8,128)S(1)} %get-tuple-element.32.refs_0_, f32[3,128,128]{2,1,0:T(8,128)S(1)} %get-tuple-element.33.refs_1_, ...), custom_call_target="tpu_custom_call" | custom-call | tf_op jit(solution)/shard_map/pallas_call | solution.py:22
  43.6 1.1 %collective-permute-start.12 = (s32[200,128]{1,0:T(8,128)S(1)}, s32[200,128]{1,0:T(8,128)S(1)}, u32[]{:S(2)}, u32[]{:S(2)}) collective-permute-start(s32[200,128]{1,0:T(8,128)S(1)} %get-tuple-element.39), channel_id=1, source_target_pairs={{0,6},{2,4},{4,2},{6,0},{8,14},{10,12},{12,10},{14,8},{16,22},{18,... | collective-permute-start | bytes 307208 | tf_op jit(solution)/shard_map/ppermute | solution.py:34
  44.7 0.9 %collective-permute-start.13 = (s32[200,128]{1,0:T(8,128)S(1)}, s32[200,128]{1,0:T(8,128)S(1)}, u32[]{:S(2)}, u32[]{:S(2)}) collective-permute-start(s32[200,128]{1,0:T(8,128)S(1)} %get-tuple-element.40), channel_id=1, source_target_pairs={{0,4},{2,6},{4,0},{6,2},{8,12},{10,14},{12,8},{14,10},{16,20},{18,... | collective-permute-start | bytes 307208 | tf_op jit(solution)/shard_map/ppermute | solution.py:34
  45.6 1.6 %collective-permute-start.14 = (s32[200,128]{1,0:T(8,128)S(1)}, s32[200,128]{1,0:T(8,128)S(1)}, u32[]{:S(2)}, u32[]{:S(2)}) collective-permute-start(s32[200,128]{1,0:T(8,128)S(1)} %get-tuple-element.41), channel_id=1, source_target_pairs={{0,2},{2,0},{4,6},{6,4},{8,10},{10,8},{12,14},{14,12},{16,18},{18,... | collective-permute-start | bytes 307208 | tf_op jit(solution)/shard_map/ppermute | solution.py:34
  47.1 1.2 %shard_map.52.refs_3_ = f32[3,512,128]{2,1,0:T(8,128)} custom-call(s32[5]{0:T(128)S(1)} %stack.23.where, f32[3,512,128]{2,1,0:T(8,128)S(1)} %get-tuple-element.27.own, f32[3,128,128]{2,1,0:T(8,128)S(1)} %get-tuple-element.42.base), custom_call_target="tpu_custom_call" | custom-call | tf_op jit(solution)/shard_map/pallas_call | solution.py:22
  48.4 0.9 %collective-permute-done.12.refs_0_ = s32[200,128]{1,0:T(8,128)S(1)} collective-permute-done((s32[200,128]{1,0:T(8,128)S(1)}, s32[200,128]{1,0:T(8,128)S(1)}, u32[]{:S(2)}, u32[]{:S(2)}) %collective-permute-start.12) | collective-permute-done | bytes 102432 | tf_op jit(solution)/shard_map/ppermute | solution.py:34
  49.3 1.0 %collective-permute-done.13.refs_1_ = s32[200,128]{1,0:T(8,128)S(1)} collective-permute-done((s32[200,128]{1,0:T(8,128)S(1)}, s32[200,128]{1,0:T(8,128)S(1)}, u32[]{:S(2)}, u32[]{:S(2)}) %collective-permute-start.13) | collective-permute-done | bytes 102432 | tf_op jit(solution)/shard_map/ppermute | solution.py:34
  50.3 1.4 %shard_map.53 = f32[3,512,128]{2,1,0:T(8,128)} custom-call(s32[5]{0:T(128)S(1)} %stack.23.where, f32[3,512,128]{2,1,0:T(8,128)S(1)} %get-tuple-element.27.own, s32[200,128]{1,0:T(8,128)S(1)} %collective-permute-done.12.refs_0_, s32[200,128]{1,0:T(8,128)S(1)} %collective-permute-done.13.refs_1_, ...), custom_call_target="tpu_custom_call", output_to_operand_aliasing={{}: (5, {})} | custom-call | tf_op jit(solution)/shard_map/pallas_call | solution.py:256
  (14 shorter events, 0.1 us)
Async XLA Ops:
  1.1 18.2 %collective-permute-start = (bf16[2,1024,128]{2,1,0:T(8,128)(2,1)S(1)}, bf16[2,1024,128]{2,1,0:T(8,128)(2,1)S(1)}, u32[]{:S(2)}, u32[]{:S(2)}) collective-permute-start(bf16[2,1024,128]{2,1,0:T(8,128)(2,1)S(1)} %slice.3), channel_id=1, source_target_pairs={{0,30},{2,0},{4,2},{6,4},{8,6},{10,8},{12,10},{14,12},{16,14},{18,... | collective-permute-start | bytes 1572872 | tf_op jit(solution)/shard_map/ppermute | solution.py:223
  8.8 1.6 %copy-start = (bf16[1,1024,1024]{2,1,0:T(8,128)(2,1)S(1)}, bf16[1,1024,1024]{2,1,0:T(8,128)(2,1)}, u32[]{:S(2)}) copy-start(bf16[1,1024,1024]{2,1,0:T(8,128)(2,1)} %param.4) | copy-start | bytes 6291460
  10.4 1.2 %copy-start.1 = (bf16[4,1024,128]{2,1,0:T(8,128)(2,1)S(1)}, bf16[4,1024,128]{2,1,0:T(8,128)(2,1)}, u32[]{:S(2)}) copy-start(bf16[4,1024,128]{2,1,0:T(8,128)(2,1)} %own.1) | copy-start | bytes 3145732
  11.6 0.7 %copy-start.2 = (s32[1,128]{1,0:T(1,128)S(1)}, s32[1,128]{1,0:T(1,128)}, u32[]{:S(2)}) copy-start(s32[1,128]{1,0:T(1,128)} %slots.3) | copy-start | bytes 1540
  13.2 6.6 %collective-permute-start.3 = (bf16[1024,384]{1,0:T(8,128)(2,1)S(1)}, bf16[1024,384]{1,0:T(8,128)(2,1)S(1)}, u32[]{:S(2)}, u32[]{:S(2)}) collective-permute-start(bf16[1024,384]{1,0:T(8,128)(2,1)S(1)} %get-tuple-element.26.refs_2_), channel_id=1, source_target_pairs={{0,1},{1,0},{2,3},{3,2},{4,5},{5,4},{6,7},{7,6},{8,9},{9,8},{10,11... | collective-permute-start | bytes 2359304 | tf_op jit(solution)/shard_map/ppermute | solution.py:34
  13.3 6.5 %collective-permute-start.1 = (bf16[256,1024]{1,0:T(8,128)(2,1)S(1)}, bf16[256,1024]{1,0:T(8,128)(2,1)S(1)}, u32[]{:S(2)}, u32[]{:S(2)}) collective-permute-start(bf16[256,1024]{1,0:T(8,128)(2,1)S(1)} %get-tuple-element.24), channel_id=1, source_target_pairs={{0,1},{1,0},{2,3},{3,2},{4,5},{5,4},{6,7},{7,6},{8,9},{9,8},{10,11... | collective-permute-start | bytes 1572872 | tf_op jit(solution)/shard_map/ppermute | solution.py:34
  13.8 6.0 %collective-permute-start.2 = (bf16[256,1024]{1,0:T(8,128)(2,1)S(1)}, bf16[256,1024]{1,0:T(8,128)(2,1)S(1)}, u32[]{:S(2)}, u32[]{:S(2)}) collective-permute-start(bf16[256,1024]{1,0:T(8,128)(2,1)S(1)} %get-tuple-element.25), channel_id=1, source_target_pairs={{0,1},{1,0},{2,3},{3,2},{4,5},{5,4},{6,7},{7,6},{8,9},{9,8},{10,11... | collective-permute-start | bytes 1572872 | tf_op jit(solution)/shard_map/ppermute | solution.py:34
  19.2 2.5 %collective-permute-start.4 = (bf16[2,1024,128]{2,1,0:T(8,128)(2,1)S(1)}, bf16[2,1024,128]{2,1,0:T(8,128)(2,1)S(1)}, u32[]{:S(2)}, u32[]{:S(2)}) collective-permute-start(bf16[2,1024,128]{2,1,0:T(8,128)(2,1)S(1)} %collective-permute-done.newer), channel_id=1, source_target_pairs={{0,1},{1,0},{2,3},{3,2},{4,5},{5,4},{6,7},{7,6},{8,9},{9,8},{10,11... | collective-permute-start | bytes 1572872 | tf_op jit(solution)/shard_map/ppermute | solution.py:34
  19.3 2.5 %collective-permute-start.5 = (s32[1,128]{1,0:T(1,128)S(1)}, s32[1,128]{1,0:T(1,128)S(1)}, u32[]{:S(2)}, u32[]{:S(2)}) collective-permute-start(s32[1,128]{1,0:T(1,128)S(1)} %copy-done.2), channel_id=1, source_target_pairs={{0,1},{1,0},{2,3},{3,2},{4,5},{5,4},{6,7},{7,6},{8,9},{9,8},{10,11... | collective-permute-start | bytes 1544 | tf_op jit(solution)/shard_map/ppermute | solution.py:34
  23.1 6.7 %collective-permute-start.6 = (s32[200,128]{1,0:T(8,128)S(1)}, s32[200,128]{1,0:T(8,128)S(1)}, u32[]{:S(2)}, u32[]{:S(2)}) collective-permute-start(s32[200,128]{1,0:T(8,128)S(1)} %get-tuple-element.29), channel_id=1, source_target_pairs={{0,6},{2,4},{4,2},{6,0},{8,14},{10,12},{12,10},{14,8},{16,22},{18,... | collective-permute-start | bytes 307208 | tf_op jit(solution)/shard_map/ppermute | solution.py:34
  24.4 6.6 %collective-permute-start.7 = (s32[200,128]{1,0:T(8,128)S(1)}, s32[200,128]{1,0:T(8,128)S(1)}, u32[]{:S(2)}, u32[]{:S(2)}) collective-permute-start(s32[200,128]{1,0:T(8,128)S(1)} %get-tuple-element.30), channel_id=1, source_target_pairs={{0,4},{2,6},{4,0},{6,2},{8,12},{10,14},{12,8},{14,10},{16,20},{18,... | collective-permute-start | bytes 307208 | tf_op jit(solution)/shard_map/ppermute | solution.py:34
  24.4 6.6 %collective-permute-start.8 = (s32[200,128]{1,0:T(8,128)S(1)}, s32[200,128]{1,0:T(8,128)S(1)}, u32[]{:S(2)}, u32[]{:S(2)}) collective-permute-start(s32[200,128]{1,0:T(8,128)S(1)} %get-tuple-element.31), channel_id=1, source_target_pairs={{0,2},{2,0},{4,6},{6,4},{8,10},{10,8},{12,14},{14,12},{16,18},{18,... | collective-permute-start | bytes 307208 | tf_op jit(solution)/shard_map/ppermute | solution.py:34
  31.2 11.1 %collective-permute-start.10 = (s32[200,128]{1,0:T(8,128)S(1)}, s32[200,128]{1,0:T(8,128)S(1)}, u32[]{:S(2)}, u32[]{:S(2)}) collective-permute-start(s32[200,128]{1,0:T(8,128)S(1)} %get-tuple-element.37), channel_id=1, source_target_pairs={{0,16},{2,18},{4,20},{6,22},{8,24},{10,26},{12,28},{14,30},{16,0},... | collective-permute-start | bytes 307208 | tf_op jit(solution)/shard_map/ppermute | solution.py:244
  32.5 9.8 %collective-permute-start.11 = (s32[200,128]{1,0:T(8,128)S(1)}, s32[200,128]{1,0:T(8,128)S(1)}, u32[]{:S(2)}, u32[]{:S(2)}) collective-permute-start(s32[200,128]{1,0:T(8,128)S(1)} %get-tuple-element.38), channel_id=1, source_target_pairs={{0,8},{2,10},{4,12},{6,14},{8,16},{10,18},{12,20},{14,22},{16,24},... | collective-permute-start | bytes 307208 | tf_op jit(solution)/shard_map/ppermute | solution.py:244
  35.8 6.9 %collective-permute-start.9 = (s32[200,128]{1,0:T(8,128)S(1)}, s32[200,128]{1,0:T(8,128)S(1)}, u32[]{:S(2)}, u32[]{:S(2)}) collective-permute-start(s32[200,128]{1,0:T(8,128)S(1)} %get-tuple-element.36), channel_id=1, source_target_pairs={{0,24},{2,26},{4,28},{6,30},{8,0},{10,2},{12,4},{14,6},{16,8},{18,... | collective-permute-start | bytes 307208 | tf_op jit(solution)/shard_map/ppermute | solution.py:244
  43.6 5.7 %collective-permute-start.12 = (s32[200,128]{1,0:T(8,128)S(1)}, s32[200,128]{1,0:T(8,128)S(1)}, u32[]{:S(2)}, u32[]{:S(2)}) collective-permute-start(s32[200,128]{1,0:T(8,128)S(1)} %get-tuple-element.39), channel_id=1, source_target_pairs={{0,6},{2,4},{4,2},{6,0},{8,14},{10,12},{12,10},{14,8},{16,22},{18,... | collective-permute-start | bytes 307208 | tf_op jit(solution)/shard_map/ppermute | solution.py:34
  44.7 5.6 %collective-permute-start.13 = (s32[200,128]{1,0:T(8,128)S(1)}, s32[200,128]{1,0:T(8,128)S(1)}, u32[]{:S(2)}, u32[]{:S(2)}) collective-permute-start(s32[200,128]{1,0:T(8,128)S(1)} %get-tuple-element.40), channel_id=1, source_target_pairs={{0,4},{2,6},{4,0},{6,2},{8,12},{10,14},{12,8},{14,10},{16,20},{18,... | collective-permute-start | bytes 307208 | tf_op jit(solution)/shard_map/ppermute | solution.py:34
  45.6 4.7 %collective-permute-start.14 = (s32[200,128]{1,0:T(8,128)S(1)}, s32[200,128]{1,0:T(8,128)S(1)}, u32[]{:S(2)}, u32[]{:S(2)}) collective-permute-start(s32[200,128]{1,0:T(8,128)S(1)} %get-tuple-element.41), channel_id=1, source_target_pairs={{0,2},{2,0},{4,6},{6,4},{8,10},{10,8},{12,14},{14,12},{16,18},{18,... | collective-permute-start | bytes 307208 | tf_op jit(solution)/shard_map/ppermute | solution.py:34
